TPU v7x, 32 devices: a whole 2x2x4 slice. The times are simulated.
32 devices in a mesh: grp: 2 (over x), tp: 8 (over z, y), dp: 2 (over core).
Axes of the slice: x: 2, y: 2, z: 4, core: 2. Of those that a mesh axis runs over, the one named last changes fastest.
Arguments:
- tokens: bfloat16 [512, 4096], P(('grp', 'dp'), 'tp'), parts along dimension 0, may hold values from -6 to 6
- cotangent: bfloat16 [512, 4096], P(('grp', 'dp'), 'tp'), parts along dimension 0, may hold values from -6 to 6
- w_gate: bfloat16 [4096, 16384], P('dp', 'tp'), may hold values from -0.09375 to 0.09375
- w_up: bfloat16 [4096, 16384], P('dp', 'tp'), may hold values from -0.09375 to 0.09375
- w_down: bfloat16 [16384, 4096], P('tp', 'dp'), may hold values from -0.046875 to 0.046875
- gate_mask: int32 [32, 128], P(None, 'tp'), may hold values from 0 to 1, as said below
- up_mask: int32 [32, 128], P(None, 'tp'), may hold values from 0 to 1, as said below
- down_mask: int32 [128, 32], P('tp'), may hold values from 0 to 1, as said below
Outputs:
- layer_out: bfloat16 [512, 4096], P(('grp', 'dp'), 'tp'), parts along dimension 0
- input_grad: bfloat16 [512, 4096], P(('grp', 'dp'), 'tp'), parts along dimension 0
- gate_grad: bfloat16 [8192, 16384], P(('grp', 'dp'), 'tp'), parts along dimension 0
- up_grad: bfloat16 [8192, 16384], P(('grp', 'dp'), 'tp'), parts along dimension 0
- down_grad: bfloat16 [32768, 4096], P(('grp', 'tp'), 'dp'), parts along dimension 0
There are 2 independent parts, one for each index of `grp`. A program takes and returns all parts, laid end to end along the dimension named above; an argument that names none is the same for every part. Nothing has to cross between parts.
Inputs may be any that keep to these rules, and one draw needn't show every extreme that they name: `gate_mask`: 1 keeps a 128 x 128 block of the weight, 0 sets it to zero. `up_mask`: 1 keeps a 128 x 128 block of the weight, 0 sets it to zero. `down_mask`: 1 keeps a 128 x 128 block of the weight, 0 sets it to zero.
All inputs are finite; a program needn't handle non-finite values.
Results may differ from a plain program's by a relative error of at most 0.0059.
Values may be sent and summed in bfloat16 or wider, within the bound.
No kernel may reach another device: no remote copies, remote signals or barrier semaphores. Data moves between devices by JAX's collectives and lax.ppermute only.
A program may use at most 320 MiB of HBM per device.

v0:
```python
import functools

import jax
import jax.numpy as jnp
from jax import lax
from jax.experimental import pallas as pl
from jax.experimental.pallas import tpu as pltpu
from jax.sharding import PartitionSpec as P

BLK = 128
BF16 = jnp.bfloat16
F32 = jnp.float32
NN = (((1,), (0,)), ((), ()))
NT = (((1,), (1,)), ((), ()))


def dot(left, right, dims):
    return lax.dot_general(left, right, dims, preferred_element_type=F32)


def masked(weight, keep):
    rows, cols = weight.shape
    kept = weight.reshape(rows // BLK, BLK, cols) * keep.astype(weight.dtype)
    return kept.reshape(rows, cols)


def whole(x):
    return pl.BlockSpec(x.shape, lambda i: (0,) * len(x.shape))


def in_hbm(x):
    return pltpu.with_memory_space_constraint(x, pltpu.HBM)


def call(body, sel, far, held, arrays, out_shape, scratch, flops, name, limit):
    return pl.pallas_call(
        body,
        grid=(1,),
        in_specs=[pl.BlockSpec(memory_space=pltpu.SMEM)]
        + [pl.BlockSpec(memory_space=pl.ANY)] * len(far)
        + [pl.BlockSpec(memory_space=pltpu.VMEM)] * len(held)
        + [whole(x) for x in arrays],
        out_specs=[whole(x) for x in out_shape],
        out_shape=out_shape,
        scratch_shapes=scratch,
        compiler_params=pltpu.CompilerParams(vmem_limit_bytes=limit * 1024 * 1024),
        cost_estimate=pl.CostEstimate(flops=flops, bytes_accessed=flops // 256, transcendentals=0),
        name=name,
    )(
        sel,
        *[in_hbm(x) for x in far],
        *[pltpu.with_memory_space_constraint(x, pltpu.VMEM) for x in held],
        *arrays,
    )


def prepare_body(weight, keep, out):
    rows = weight.shape[0]
    first = pl.multiple_of(pl.program_id(0) * rows, rows)
    out[pl.ds(first, rows), :] = masked(weight[...], keep[...])


def prepare(weight, keep, name):
    rows, cols = weight.shape
    tile = min(1024, rows)
    return pl.pallas_call(
        prepare_body,
        grid=(rows // tile,),
        in_specs=[
            pl.BlockSpec((tile, cols), lambda i: (i, 0)),
            pl.BlockSpec((tile // BLK, 1, cols), lambda i: (i, 0, 0)),
        ],
        out_specs=pl.BlockSpec(memory_space=pltpu.VMEM),
        out_shape=pltpu.VMEM((rows, cols), weight.dtype),
        compiler_params=pltpu.CompilerParams(vmem_limit_bytes=14 * 1024 * 1024),
        cost_estimate=pl.CostEstimate(flops=0, bytes_accessed=rows * cols // 16, transcendentals=0),
        name=name,
    )(in_hbm(weight), keep)


class Stream:
    def __init__(self, weights, buffers, sems, places):
        self.copies = []
        for c, (place, slot) in enumerate(places):
            for i, (weight, buffer) in enumerate(zip(weights, buffers)):
                self.copies.append(
                    pltpu.make_async_copy(weight.at[place], buffer.at[slot], sems.at[i, c])
                )
        for copy in self.copies:
            copy.start()
        self.step, self.count = 0, len(weights)

    def wait(self):
        for copy in self.copies[self.step : self.step + self.count]:
            copy.wait()
        self.step += self.count


def tiles(size, tile=512):
    tile = min(tile, size)
    return [slice(first, first + tile) for first in range(0, size, tile)]


def collect(pieces, refs, lhs, sel, half):
    feats = lhs.shape[1] // half
    for (block, near), ref in zip(pieces, refs):
        place = pl.ds(pl.multiple_of((block ^ sel[0]) * feats, feats), feats)

        def put(ref=ref, place=place):
            lhs[:, place] = ref[...]

        if near is None:
            put()
        else:
            pl.when(sel[1] == near)(put)


def shapes(rows, cols, *types):
    return [jax.ShapeDtypeStruct((rows, cols), kind) for kind in types]


def late(rows, cols):
    return [pltpu.HBM((rows, cols), BF16)]


def of_blocks(part):
    return slice(part.start // BLK, part.stop // BLK)


def forward_body(pieces, half, sel, wg, wu, mg, mu, *refs):
    blocks, refs = refs[: len(pieces)], refs[len(pieces) :]
    gate, up, lhs, wg_buf, wu_buf, sum_gate, sum_up, sems = refs
    deep = tiles(wg.shape[0])
    stream = Stream((wg, wu), (wg_buf, wu_buf), sems, [(rows, rows) for rows in deep])
    collect(pieces, blocks, lhs, sel, half)
    for step, rows in enumerate(deep):
        stream.wait()
        for buf, keep, total, out in ((wg_buf, mg, sum_gate, gate), (wu_buf, mu, sum_up, up)):
            for cols in tiles(out.shape[1]):
                weight = masked(buf[rows, cols], keep[of_blocks(rows), :, cols])
                part = dot(lhs[:, rows], weight, NN)
                if step > 0:
                    part = part + total[:, cols]
                if step < len(deep) - 1:
                    total[:, cols] = part
                else:
                    out[:, cols] = part.astype(BF16)


def forward(sel, got, w_gate, w_up, keep_gate, keep_up, half, rows):
    pieces, blocks = zip(*got)
    depth, width = w_gate.shape
    return call(
        functools.partial(forward_body, pieces, half),
        sel,
        [w_gate, w_up],
        [],
        [keep_gate, keep_up, *blocks],
        shapes(rows, width, BF16, BF16) + late(rows, depth),
        [pltpu.VMEM((depth, width), BF16)] * 2
        + [pltpu.VMEM((rows, width), F32)] * 2
        + [pltpu.SemaphoreType.DMA((2, 16))],
        rows * depth * width // 16,
        "forward",
        30,
    )


def middle_body(pieces, half, sel, weight, *refs):
    count = len(pieces)
    blocks, sums, refs = refs[:count], refs[count : count + 4], refs[count + 4 :]
    (grad, lhs, hidden, by_gate, by_up), outs = refs[:5], refs[5:]
    for cols in tiles(hidden.shape[1]):
        gate, up = add(sums[:2], cols), add(sums[2:], cols)
        sig = jax.nn.sigmoid(gate)
        silu = gate * sig
        hidden[:, cols] = (silu * up).astype(BF16)
        by_gate[:, cols] = up * sig * (1.0 + gate * (1.0 - sig))
        by_up[:, cols] = silu
    for out, place in zip(outs, places_of(range(half), sel, outs[0].shape[1])):
        out[...] = dot(hidden[...], weight[:, place], NN).astype(BF16)
    collect(pieces, blocks, lhs, sel, half)
    for cols in tiles(weight.shape[0]):
        grad[:, cols] = dot(lhs[...], weight[cols], NT).astype(BF16)


def middle(sel, got, sums, w_down, half, rows):
    pieces, blocks = zip(*got)
    width, depth = w_down.shape
    return call(
        functools.partial(middle_body, pieces, half),
        sel,
        [],
        [w_down],
        [*blocks, *sums],
        shapes(rows, width, BF16)
        + late(rows, depth)
        + late(rows, width)
        + shapes(rows, width, F32, F32)
        + late(rows, depth // half) * half,
        [],
        4 * rows * depth * width,
        "middle",
        20,
    )


def places_of(wanted, sel, feats):
    return [pl.ds(pl.multiple_of((j ^ sel[0]) * feats, feats), feats) for j in wanted]


def add(pair, cols):
    return pair[0][:, cols].astype(F32) + pair[1][:, cols].astype(F32)


def delta_tile(arrays, cols):
    by_gate, by_up, *grads = arrays
    grad = add(grads, cols)
    return (grad * by_gate[:, cols]).astype(BF16), (grad * by_up[:, cols]).astype(BF16)


def product_body(wanted, make, count, made, sel, *refs):
    sides = 2
    weights, refs = refs[:sides], refs[sides:]
    keeps, refs = refs[:sides], refs[sides:]
    arrays, refs = refs[:count], refs[count:]
    blocks, refs = refs[: len(wanted)], refs[len(wanted) :]
    lefts, refs = (refs[:made], refs[made:]) if make else (arrays, refs)
    buffers, sems = refs[:sides], refs[sides]
    feats = blocks[0].shape[1]
    kept = feats // BLK
    places = places_of(wanted, sel, feats)
    slots = [pl.ds(i * feats, feats) for i in range(len(wanted))]
    cut = lambda place: (place, slice(None))
    stream = Stream(weights, buffers, sems, [(cut(p), cut(q)) for p, q in zip(places, slots)])
    if make:
        for cols in tiles(lefts[0].shape[1]):
            for left, value in zip(lefts, make(arrays, cols)):
                left[:, cols] = value
    for j, place, slot, block in zip(wanted, places, slots, blocks):
        stream.wait()
        total = None
        for left, buffer, keep in zip(lefts, buffers, keeps):
            weight = masked(buffer[slot, :], keep[pl.ds((j ^ sel[0]) * kept, kept)])
            part = dot(left[...], weight, NT)
            total = part if total is None else total + part
        block[...] = total.astype(BF16)


def product(sel, wanted, make, arrays, weights, keeps, half, name):
    rows, width = arrays[0].shape
    depth = weights[0].size // width
    feats = depth // half
    made = len(weights) if make else 0
    held = len(wanted) * feats
    return call(
        functools.partial(product_body, wanted, make, len(arrays), made),
        sel,
        weights,
        [],
        [*keeps, *arrays],
        shapes(rows, feats, BF16) * len(wanted) + shapes(rows, width, BF16) * made,
        [pltpu.VMEM((held, width), BF16)] * 2 + [pltpu.SemaphoreType.DMA((2, len(wanted)))],
        2 * rows * held * width * len(weights),
        name,
        12 + len(weights) * held * width // 2**19,
    )


def weight_grad_body(left, right, keep, out):
    rows, cols = out.shape
    term = dot(left[...].T, right[...], NN).reshape(rows // BLK, BLK, cols) * keep[...]
    out[...] = term.reshape(rows, cols).astype(BF16)


def weight_grad(left, right, keep, name):
    rows, height = left.shape
    width = right.shape[1]
    tile = min(512, height)
    flops = 2 * rows * height * width
    return pl.pallas_call(
        weight_grad_body,
        grid=(height // tile,),
        in_specs=[
            pl.BlockSpec((rows, tile), lambda i: (0, i)),
            pl.BlockSpec((rows, width), lambda i: (0, 0)),
            pl.BlockSpec((tile // BLK, 1, width), lambda i: (i, 0, 0)),
        ],
        out_specs=pl.BlockSpec((tile, width), lambda i: (i, 0)),
        out_shape=jax.ShapeDtypeStruct((height, width), BF16),
        compiler_params=pltpu.CompilerParams(vmem_limit_bytes=16 * 1024 * 1024),
        cost_estimate=pl.CostEstimate(flops=flops, bytes_accessed=flops // 256, transcendentals=0),
        name=name,
    )(left, right, keep)


def expand_cols(block_mask):
    rows, cols = block_mask.shape
    grown = jnp.broadcast_to(block_mask[:, :, None], (rows, cols, BLK)).astype(F32)
    return grown.reshape(rows, 1, cols * BLK)


def permute(x, route):
    return lax.ppermute(x, ("tp", "dp"), route)


def back(route):
    return [(target, source) for source, target in route]


def swap(part):
    return lax.ppermute(part, "dp", [(0, 1), (1, 0)])


def direct_routes(n):
    half = n // 2
    for k in range(n):
        yield [
            (t * 2 + core, ((((core ^ (k // half)) * half) + ((t % half) ^ (k % half))) * 2 + t // half))
            for t in range(n)
            for core in range(2)
        ]


def direct_gather(block, n):
    half, rows = n // 2, block.shape[0]
    run = lax.axis_index("tp") // half
    got = [permute(block, route) for route in direct_routes(n)]
    pieces = []
    for j in range(half):
        both = jnp.where(
            run == 0,
            jnp.concatenate((got[j], got[half + j])),
            jnp.concatenate((got[half + j], got[j])),
        )
        pieces.append(((j, None), both))
    return pieces


def direct_scatter(blocks, n):
    half, rows = n // 2, blocks[0].shape[0] // 2
    run = lax.axis_index("tp") // half
    total = None
    for k, route in enumerate(direct_routes(n)):
        first = (run ^ (k // half)) * rows
        block = lax.dynamic_slice_in_dim(blocks[k % half], first, rows, 0)
        got = permute(block, back(route)).astype(F32)
        total = got if total is None else total + got
    return total.astype(BF16)


def staged_routes():
    names = ("near", "far", "across", "across_near", "across_far")
    pairs = {name: [] for name in names}
    for z in range(4):
        for y in range(2):
            for core in range(2):
                want = z // 2
                me = (z * 2 + y) * 2 + core
                at = lambda to_z, to_y, to_core: (to_z * 2 + to_y) * 2 + to_core
                pairs["near"].append((me, at(z ^ 1 if core == want else z ^ 3, y, want)))
                if core != want:
                    pairs["far"].append((me, at(z ^ 2, y, want)))
                pairs["across"].append((me, at(z, y ^ 1, core)))
                kind = "across_near" if core == want else "across_far"
                pairs[kind].append((me, at(z, y ^ 1, core)))
    return pairs


def after(x, *others):
    return lax.optimization_barrier((x, *others))[0]


def of_chip(block):
    other = swap(block)
    first = lax.axis_index("dp") == 0
    return jnp.concatenate((jnp.where(first, block, other), jnp.where(first, other, block)))


def staged_gathers(tokens, cotangent, near):
    routes = staged_routes()
    chip = of_chip(tokens)
    cot_chip = of_chip(after(cotangent, chip))
    one = permute(chip, routes["near"])
    two = permute(chip, routes["far"])
    beside = permute(chip, routes["across_near"])
    cot_one = permute(cot_chip, routes["near"])
    cot_here = jnp.where(near, cot_chip, permute(cot_chip, routes["far"]))
    one, two = after(one, cot_chip), after(two, cot_chip)
    tok_blocks = [
        ((0, 1), after(chip, cot_one, cot_here)),
        ((0, 0), two),
        ((2, None), one),
        ((1, 1), beside),
        ((3, None), permute(one, routes["across"])),
        ((1, 0), permute(two, routes["across_far"])),
    ]
    cot_blocks = [
        ((0, None), cot_here),
        ((2, None), cot_one),
        ((3, None), permute(cot_one, routes["across"])),
        ((1, None), permute(cot_here, routes["across"])),
    ]
    return tok_blocks, cot_blocks


def staged_across(blocks):
    across = staged_routes()["across"]
    return [permute(block, across) for block in blocks]


def staged_halves(blocks, got):
    return [
        (block.astype(F32) + other.astype(F32)).astype(BF16) for block, other in zip(blocks, got)
    ]


def staged_route(halves):
    routes = staged_routes()
    two, one = halves
    return permute(one, back(routes["near"])), permute(two, back(routes["far"]))


def staged_finish(halves, got, near):
    one, two = got
    total = one.astype(F32) + jnp.where(near, halves[0], two).astype(F32)
    rows = total.shape[0] // 2
    core = lax.axis_index("dp")
    theirs = lax.dynamic_slice_in_dim(total, (1 - core) * rows, rows, 0)
    mine = lax.dynamic_slice_in_dim(total, core * rows, rows, 0)
    return (mine + swap(theirs.astype(BF16)).astype(F32)).astype(BF16)


def shards(tokens, cotangent, w_gate, w_up, w_down, gate_mask, up_mask, down_mask):
    n = lax.axis_size("tp")
    half = n // 2
    rows = 2 * tokens.shape[0]
    at, core = lax.axis_index("tp"), lax.axis_index("dp")
    near = (at // half) == core
    sel = jnp.stack((at % half, near.astype(jnp.int32))).astype(jnp.int32)
    half_rows = w_gate.shape[0] // BLK
    offset = core * half_rows
    keep_gate = expand_cols(lax.dynamic_slice_in_dim(gate_mask, offset, half_rows, 0))
    keep_up = expand_cols(lax.dynamic_slice_in_dim(up_mask, offset, half_rows, 0))
    keep_down = expand_cols(lax.dynamic_slice_in_dim(down_mask, offset, half_rows, 1))

    staged = n == 8
    if staged:
        tok_blocks, cot_blocks = staged_gathers(tokens, cotangent, near)
    else:
        tok_blocks, cot_blocks = direct_gather(tokens, n), direct_gather(cotangent, n)
    gate, up, tok = forward(sel, tok_blocks, w_gate, w_up, keep_gate, keep_up, half, rows)
    late_up = after(up, *[block for _, block in cot_blocks[2:]]) if staged else up
    sums = [gate, swap(gate), up, swap(late_up)]
    w_held = prepare(w_down, after(keep_down, gate), "prepare_down")
    grad, cot, hidden, by_gate, by_up, *out_blocks = middle(
        sel, cot_blocks, sums, w_held, half, rows
    )
    deltas = [by_gate, by_up, grad, swap(grad)]
    gate_up = lambda wanted, make, arrays, name: product(
        sel, wanted, make, arrays, [w_gate, w_up], [keep_gate, keep_up], half, name
    )
    if staged:
        out_got = staged_across((out_blocks[1], out_blocks[3]))
        in_1, gate_delta, up_delta = gate_up((1,), delta_tile, deltas, "input_first")
        in_3, in_0, in_2 = gate_up((3, 0, 2), None, [gate_delta, up_delta], "input_rest")
        gate_grad = weight_grad(after(tok, in_0), gate_delta, keep_gate, "gate_grad")
        in_got = [after(x, gate_grad) for x in staged_across((in_1, in_3))]
        in_two = staged_halves((in_0,), in_got[:1])
        out_got = [after(x, *in_two) for x in out_got]
        out_halves = staged_halves((out_blocks[0], out_blocks[2]), out_got)
        up_grad = weight_grad(tok, after(up_delta, *out_halves), keep_up, "up_grad")
        in_halves = in_two + staged_halves((in_2,), [after(in_got[1], up_grad)])
        down_grad = weight_grad(hidden, after(cot, *in_halves), keep_down, "down_grad")
        layer_out = staged_finish(out_halves, staged_route(out_halves), near)
        input_grad = staged_finish(in_halves, staged_route(in_halves), near)
    else:
        *in_blocks, gate_delta, up_delta = gate_up(range(half), delta_tile, deltas, "input_grads")
        gate_grad = weight_grad(tok, gate_delta, keep_gate, "gate_grad")
        up_grad = weight_grad(tok, up_delta, keep_up, "up_grad")
        down_grad = weight_grad(hidden, cot, keep_down, "down_grad")
        layer_out, input_grad = direct_scatter(out_blocks, n), direct_scatter(in_blocks, n)
    return layer_out, input_grad, gate_grad, up_grad, down_grad


def solution(mesh):
    rows = P(("grp", "dp"), "tp")
    return jax.shard_map(
        shards,
        mesh=mesh,
        in_specs=(
            rows,
            rows,
            P("dp", "tp"),
            P("dp", "tp"),
            P("tp", "dp"),
            P(None, "tp"),
            P(None, "tp"),
            P("tp", None),
        ),
        out_specs=(rows, rows, rows, rows, P(("grp", "tp"), "dp")),
        check_vma=False,
    )
```

profile of v0, /device:TPU:19, one launch (start us, length us, event | category | flops | bytes accessed | tf_op | source)
XLA Modules:
  0.0 106.2 jit_solution(14847317135482934332)
XLA Ops:
  0.6 0.7 collective-permute-start
  1.4 1.2 %collective-permute-done = bf16[128,512]{1,0:T(8,128)(2,1)S(1)} collective-permute-done((bf16[128,512]{1,0:T(8,128)(2,1)}, bf16[128,512]{1,0:T(8,128)(2,1)S(1)}, u32[]{:S(2)}, u32[]{:S(2)}) %collective-permute-start) | collective-permute-done | bytes 131104 | tf_op jit(solution)/shard_map/ppermute | solution.py:312
  2.6 0.9 broadcast_select_fusion.4
  4.0 1.3 %collective-permute-start.5 = (bf16[256,512]{1,0:T(8,128)(2,1)S(1)}, bf16[256,512]{1,0:T(8,128)(2,1)S(1)}, u32[]{:S(2)}, u32[]{:S(2)}) collective-permute-start(bf16[256,512]{1,0:T(8,128)(2,1)S(1)} %pad_maximum_fusion.refs_0_), channel_id=1, source_target_pairs={{0,4},{1,12},{2,6},{3,14},{4,0},{5,8},{6,2},{7,10},{8,5},{9,13},{1... | collective-permute-start | bytes 786440 | tf_op jit(solution)/shard_map/ppermute | solution.py:304
  5.9 0.9 broadcast_select_fusion.2
  8.2 3.1 %collective-permute-start.6 = (bf16[256,512]{1,0:T(8,128)(2,1)S(1)}, bf16[256,512]{1,0:T(8,128)(2,1)S(1)}, u32[]{:S(2)}, u32[]{:S(2)}) collective-permute-start(bf16[256,512]{1,0:T(8,128)(2,1)S(1)} %pad_maximum_fusion.refs_0_), channel_id=1, source_target_pairs={{0,2},{2,0},{4,6},{6,4},{9,11},{11,9},{13,15},{15,13},{16,18},{18,... | collective-permute-start | bytes 786440 | tf_op jit(solution)/shard_map/ppermute | solution.py:304
  11.7 1.2 %collective-permute-start.7 = (bf16[256,512]{1,0:T(8,128)(2,1)S(1)}, bf16[256,512]{1,0:T(8,128)(2,1)S(1)}, u32[]{:S(2)}, u32[]{:S(2)}) collective-permute-start(bf16[256,512]{1,0:T(8,128)(2,1)S(1)} %collective-permute-done.5.refs_2_), channel_id=1, source_target_pairs={{0,2},{1,3},{2,0},{3,1},{4,6},{5,7},{6,4},{7,5},{8,10},{9,11},{10,... | collective-permute-start | bytes 786440 | tf_op jit(solution)/shard_map/ppermute | solution.py:304
  14.0 3.6 %collective-permute-done.2.refs_1_ = bf16[256,512]{1,0:T(8,128)(2,1)S(1)} collective-permute-done((bf16[256,512]{1,0:T(8,128)(2,1)S(1)}, bf16[256,512]{1,0:T(8,128)(2,1)S(1)}, u32[]{:S(2)}, u32[]{:S(2)}) %collective-permute-start.2) | collective-permute-done | bytes 262176 | tf_op jit(solution)/shard_map/ppermute | solution.py:304
  17.6 1.2 %collective-permute-start.9 = (bf16[256,512]{1,0:T(8,128)(2,1)S(1)}, bf16[256,512]{1,0:T(8,128)(2,1)S(1)}, u32[]{:S(2)}, u32[]{:S(2)}) collective-permute-start(bf16[256,512]{1,0:T(8,128)(2,1)S(1)} %collective-permute-done.2.refs_1_), channel_id=1, source_target_pairs={{0,2},{1,3},{2,0},{3,1},{4,6},{5,7},{6,4},{7,5},{8,10},{9,11},{10,... | collective-permute-start | bytes 786440 | tf_op jit(solution)/shard_map/ppermute | solution.py:304
  18.9 0.8 dynamic-slice_convert_fusion.2
  20.1 8.2 %forward.1 = (bf16[256,2048]{1,0:T(8,128)(2,1)S(1)}, bf16[256,2048]{1,0:T(8,128)(2,1)S(1)}, bf16[256,2048]{1,0:T(8,128)(2,1)}) custom-call(s32[2]{0:T(128)S(1)} %pad_add_fusion.sel, bf16[2048,2048]{1,0:T(8,128)(2,1)} %refs_0_.3, bf16[2048,2048]{1,0:T(8,128)(2,1)} %refs_1_.3, f32[16,1,2048]{2,1,0:T(1,128)S(1)} %bitcast.9, f32[16,1,2048]{2,1,0:T(1,128)S(1)} %bitcast.5, ...), custom_call_target="tpu_custom_call" | custom-call | flops 67108864 | bytes 262144 | tf_op jit(solution)/shard_map/forward/pallas_call | solution.py:36
  28.4 12.3 %collective-permute-start.11 = (bf16[256,2048]{1,0:T(8,128)(2,1)S(1)}, bf16[256,2048]{1,0:T(8,128)(2,1)S(1)}, u32[]{:S(2)}, u32[]{:S(2)}) collective-permute-start(bf16[256,2048]{1,0:T(8,128)(2,1)S(1)} %get-tuple-element.41.refs_4_), channel_id=1, source_target_pairs={{0,1},{1,0},{2,3},{3,2},{4,5},{5,4},{6,7},{7,6},{8,9},{9,8},{10,11... | collective-permute-start | bytes 3145736 | tf_op jit(solution)/shard_map/ppermute | solution.py:312
  40.7 0.7 copy-done.9
  41.6 4.0 %prepare_down.1.weight = bf16[2048,2048]{1,0:T(8,128)(2,1)S(1)} custom-call(bf16[2048,2048]{1,0:T(8,128)(2,1)} %weight.1, f32[16,1,2048]{2,1,0:T(1,128)S(1)} %bitcast.13), custom_call_target="tpu_custom_call" | custom-call | bytes 262144 | tf_op jit(solution)/shard_map/prepare_down/pallas_call | solution.py:66
  45.7 0.9 copy-done.12
  46.7 7.0 %middle.1 = (bf16[256,2048]{1,0:T(8,128)(2,1)S(1)}, bf16[256,2048]{1,0:T(8,128)(2,1)}, bf16[256,2048]{1,0:T(8,128)(2,1)}, f32[256,2048]{1,0:T(8,128)S(1)}, f32[2...) custom-call(s32[2]{0:T(128)S(1)} %pad_add_fusion.sel, ...), custom_call_target="tpu_custom_call" | custom-call | flops 4294967296 | bytes 16777216 | tf_op jit(solution)/shard_map/middle/pallas_call | solution.py:36
  53.6 1.3 %copy-done.1 = f32[256,2048]{1,0:T(8,128)} copy-done((f32[256,2048]{1,0:T(8,128)}, f32[256,2048]{1,0:T(8,128)S(1)}, u32[]{:S(2)}) %copy-start.1) | copy-done | bytes 2097176
  55.7 1.2 %collective-permute-start.17 = (bf16[256,512]{1,0:T(8,128)(2,1)}, bf16[256,512]{1,0:T(8,128)(2,1)S(1)}, u32[]{:S(2)}, u32[]{:S(2)}) collective-permute-start(bf16[256,512]{1,0:T(8,128)(2,1)} %get-tuple-element.59), channel_id=1, source_target_pairs={{0,2},{1,3},{2,0},{3,1},{4,6},{5,7},{6,4},{7,5},{8,10},{9,11},{10,... | collective-permute-start | bytes 786440 | tf_op jit(solution)/shard_map/ppermute | solution.py:304
  56.9 1.0 collective-permute-done.14.refs_7_
  57.9 1.6 %copy-done.2 = f32[256,2048]{1,0:T(8,128)S(1)} copy-done((f32[256,2048]{1,0:T(8,128)S(1)}, f32[256,2048]{1,0:T(8,128)}, u32[]{:S(2)}) %copy-start.2) | copy-done | bytes 2097176
  59.4 4.9 %input_first.1 = (bf16[256,512]{1,0:T(8,128)(2,1)S(1)}, bf16[256,2048]{1,0:T(8,128)(2,1)S(1)}, bf16[256,2048]{1,0:T(8,128)(2,1)S(1)}) custom-call(s32[2]{0:T(128)S(1)} %pad_add_fusion.sel, bf16[2048,2048]{1,0:T(8,128)(2,1)} %refs_0_.3, bf16[2048,2048]{1,0:T(8,128)(2,1)} %refs_1_.3, f32[16,1,2048]{2,1,0:T(1,128)S(1)} %bitcast.10, f32[16,1,2048]{2,1,0:T(1,128)S(1)} %bitcast.6, ...), custom_call_target="tpu_custom_call" | custom-call | flops 1073741824 | bytes 4194304 | tf_op jit(solution)/shard_map/input_first/pallas_call | solution.py:36
  64.7 7.1 %input_rest.1 = (bf16[256,512]{1,0:T(8,128)(2,1)S(1)}, bf16[256,512]{1,0:T(8,128)(2,1)S(1)}, bf16[256,512]{1,0:T(8,128)(2,1)S(1)}) custom-call(s32[2]{0:T(128)S(1)} %pad_add_fusion.sel, bf16[2048,2048]{1,0:T(8,128)(2,1)} %refs_0_.3, bf16[2048,2048]{1,0:T(8,128)(2,1)} %refs_1_.3, f32[16,1,2048]{2,1,0:T(1,128)S(1)} %bitcast.11, f32[16,1,2048]{2,1,0:T(1,128)S(1)} %bitcast.7, ...), custom_call_target="tpu_custom_call" | custom-call | flops 3221225472 | bytes 12582912 | tf_op jit(solution)/shard_map/input_rest/pallas_call | solution.py:36
  71.8 1.3 %collective-permute-start.20 = (bf16[256,512]{1,0:T(8,128)(2,1)S(1)}, bf16[256,512]{1,0:T(8,128)(2,1)S(1)}, u32[]{:S(2)}, u32[]{:S(2)}) collective-permute-start(bf16[256,512]{1,0:T(8,128)(2,1)S(1)} %get-tuple-element.62), channel_id=1, source_target_pairs={{0,2},{1,3},{2,0},{3,1},{4,6},{5,7},{6,4},{7,5},{8,10},{9,11},{10,... | collective-permute-start | bytes 786440 | tf_op jit(solution)/shard_map/ppermute | solution.py:304
  73.1 5.0 %gate_grad.1 = bf16[2048,2048]{1,0:T(8,128)(2,1)} custom-call(bf16[256,2048]{1,0:T(8,128)(2,1)S(1)} %copy-done, bf16[256,2048]{1,0:T(8,128)(2,1)S(1)} %get-tuple-element.50.refs_4_.right, f32[16,1,2048]{2,1,0:T(1,128)S(1)} %bitcast.12), custom_call_target="tpu_custom_call" | custom-call | flops 2147483648 | bytes 8388608 | tf_op jit(solution)/shard_map/gate_grad/pallas_call | solution.py:281
  78.4 0.8 collective-permute-start.18
  80.3 5.0 %up_grad.1 = bf16[2048,2048]{1,0:T(8,128)(2,1)} custom-call(bf16[256,2048]{1,0:T(8,128)(2,1)S(1)} %copy-done, bf16[256,2048]{1,0:T(8,128)(2,1)S(1)} %get-tuple-element.64.refs_5_.right, f32[16,1,2048]{2,1,0:T(1,128)S(1)} %bitcast.8), custom_call_target="tpu_custom_call" | custom-call | flops 2147483648 | bytes 8388608 | tf_op jit(solution)/shard_map/up_grad/pallas_call | solution.py:281
  85.3 1.1 %collective-permute-start.21 = (bf16[256,512]{1,0:T(8,128)(2,1)S(1)}, bf16[256,512]{1,0:T(8,128)(2,1)S(1)}, u32[]{:S(2)}, u32[]{:S(2)}) collective-permute-start(bf16[256,512]{1,0:T(8,128)(2,1)S(1)} %add_convert_fusion), channel_id=1, source_target_pairs={{4,0},{12,1},{6,2},{14,3},{0,4},{8,5},{2,6},{10,7},{5,8},{13,9},{7... | collective-permute-start | bytes 786440 | tf_op jit(solution)/shard_map/ppermute | solution.py:304
  86.4 4.9 %down_grad.1 = bf16[2048,2048]{1,0:T(8,128)(2,1)} custom-call(bf16[256,2048]{1,0:T(8,128)(2,1)S(1)} %copy-done.4, bf16[256,2048]{1,0:T(8,128)(2,1)S(1)} %copy-done.3, f32[16,1,2048]{2,1,0:T(1,128)S(1)} %bitcast.14), custom_call_target="tpu_custom_call" | custom-call | flops 2147483648 | bytes 8388608 | tf_op jit(solution)/shard_map/down_grad/pallas_call | solution.py:281
  91.5 6.4 %collective-permute-start.19 = (bf16[128,512]{1,0:T(8,128)(2,1)S(1)}, bf16[128,512]{1,0:T(8,128)(2,1)S(1)}, u32[]{:S(2)}, u32[]{:S(2)}) collective-permute-start(bf16[128,512]{1,0:T(8,128)(2,1)S(1)} %dynamic-slice_convert_fusion.1), channel_id=1, source_target_pairs={{0,1},{1,0},{2,3},{3,2},{4,5},{5,4},{6,7},{7,6},{8,9},{9,8},{10,11... | collective-permute-start | bytes 393224 | tf_op jit(solution)/shard_map/ppermute | solution.py:312
  98.0 6.6 %collective-permute-start.23 = (bf16[128,512]{1,0:T(8,128)(2,1)S(1)}, bf16[128,512]{1,0:T(8,128)(2,1)S(1)}, u32[]{:S(2)}, u32[]{:S(2)}) collective-permute-start(bf16[128,512]{1,0:T(8,128)(2,1)S(1)} %dynamic-slice_convert_fusion), channel_id=1, source_target_pairs={{0,1},{1,0},{2,3},{3,2},{4,5},{5,4},{6,7},{7,6},{8,9},{9,8},{10,11... | collective-permute-start | bytes 393224 | tf_op jit(solution)/shard_map/ppermute | solution.py:312
  104.6 0.7 add_convert_fusion.5
  105.6 0.7 add_convert_fusion.4
  (79 shorter events, 7.4 us)
Async XLA Ops:
  0.6 1.9 %collective-permute-start = (bf16[128,512]{1,0:T(8,128)(2,1)}, bf16[128,512]{1,0:T(8,128)(2,1)S(1)}, u32[]{:S(2)}, u32[]{:S(2)}) collective-permute-start(bf16[128,512]{1,0:T(8,128)(2,1)} %param.8), channel_id=1, source_target_pairs={{0,1},{1,0},{2,3},{3,2},{4,5},{5,4},{6,7},{7,6},{8,9},{9,8},{10,11... | collective-permute-start | bytes 393224 | tf_op jit(solution)/shard_map/ppermute | solution.py:312
  3.5 2.4 %collective-permute-start.1 = (bf16[128,512]{1,0:T(8,128)(2,1)}, bf16[128,512]{1,0:T(8,128)(2,1)S(1)}, u32[]{:S(2)}, u32[]{:S(2)}) collective-permute-start(bf16[128,512]{1,0:T(8,128)(2,1)} %param.9), channel_id=1, source_target_pairs={{0,1},{1,0},{2,3},{3,2},{4,5},{5,4},{6,7},{7,6},{8,9},{9,8},{10,11... | collective-permute-start | bytes 393224 | tf_op jit(solution)/shard_map/ppermute | solution.py:312
  4.0 7.8 %collective-permute-start.5 = (bf16[256,512]{1,0:T(8,128)(2,1)S(1)}, bf16[256,512]{1,0:T(8,128)(2,1)S(1)}, u32[]{:S(2)}, u32[]{:S(2)}) collective-permute-start(bf16[256,512]{1,0:T(8,128)(2,1)S(1)} %pad_maximum_fusion.refs_0_), channel_id=1, source_target_pairs={{0,4},{1,12},{2,6},{3,14},{4,0},{5,8},{6,2},{7,10},{8,5},{9,13},{1... | collective-permute-start | bytes 786440 | tf_op jit(solution)/shard_map/ppermute | solution.py:304
  5.2 7.7 %collective-permute-start.4 = (bf16[256,512]{1,0:T(8,128)(2,1)S(1)}, bf16[256,512]{1,0:T(8,128)(2,1)S(1)}, u32[]{:S(2)}, u32[]{:S(2)}) collective-permute-start(bf16[256,512]{1,0:T(8,128)(2,1)S(1)} %pad_maximum_fusion.refs_0_), channel_id=1, source_target_pairs={{1,8},{3,10},{5,12},{7,14},{8,1},{10,3},{12,5},{14,7},{17,24},{19,... | collective-permute-start | bytes 786440 | tf_op jit(solution)/shard_map/ppermute | solution.py:304
  6.9 6.7 %collective-permute-start.3 = (bf16[256,512]{1,0:T(8,128)(2,1)S(1)}, bf16[256,512]{1,0:T(8,128)(2,1)S(1)}, u32[]{:S(2)}, u32[]{:S(2)}) collective-permute-start(bf16[256,512]{1,0:T(8,128)(2,1)S(1)} %pad_maximum_fusion.1), channel_id=1, source_target_pairs={{1,8},{3,10},{5,12},{7,14},{8,1},{10,3},{12,5},{14,7},{17,24},{19,... | collective-permute-start | bytes 786440 | tf_op jit(solution)/shard_map/ppermute | solution.py:304
  7.6 10.1 %collective-permute-start.2 = (bf16[256,512]{1,0:T(8,128)(2,1)S(1)}, bf16[256,512]{1,0:T(8,128)(2,1)S(1)}, u32[]{:S(2)}, u32[]{:S(2)}) collective-permute-start(bf16[256,512]{1,0:T(8,128)(2,1)S(1)} %pad_maximum_fusion.1), channel_id=1, source_target_pairs={{0,4},{1,12},{2,6},{3,14},{4,0},{5,8},{6,2},{7,10},{8,5},{9,13},{1... | collective-permute-start | bytes 786440 | tf_op jit(solution)/shard_map/ppermute | solution.py:304
  8.2 11.7 %collective-permute-start.6 = (bf16[256,512]{1,0:T(8,128)(2,1)S(1)}, bf16[256,512]{1,0:T(8,128)(2,1)S(1)}, u32[]{:S(2)}, u32[]{:S(2)}) collective-permute-start(bf16[256,512]{1,0:T(8,128)(2,1)S(1)} %pad_maximum_fusion.refs_0_), channel_id=1, source_target_pairs={{0,2},{2,0},{4,6},{6,4},{9,11},{11,9},{13,15},{15,13},{16,18},{18,... | collective-permute-start | bytes 786440 | tf_op jit(solution)/shard_map/ppermute | solution.py:304
  11.7 8.2 %collective-permute-start.7 = (bf16[256,512]{1,0:T(8,128)(2,1)S(1)}, bf16[256,512]{1,0:T(8,128)(2,1)S(1)}, u32[]{:S(2)}, u32[]{:S(2)}) collective-permute-start(bf16[256,512]{1,0:T(8,128)(2,1)S(1)} %collective-permute-done.5.refs_2_), channel_id=1, source_target_pairs={{0,2},{1,3},{2,0},{3,1},{4,6},{5,7},{6,4},{7,5},{8,10},{9,11},{10,... | collective-permute-start | bytes 786440 | tf_op jit(solution)/shard_map/ppermute | solution.py:304
  13.0 6.9 %collective-permute-start.8 = (bf16[256,512]{1,0:T(8,128)(2,1)S(1)}, bf16[256,512]{1,0:T(8,128)(2,1)S(1)}, u32[]{:S(2)}, u32[]{:S(2)}) collective-permute-start(bf16[256,512]{1,0:T(8,128)(2,1)S(1)} %collective-permute-done.4.refs_1_), channel_id=1, source_target_pairs={{1,3},{3,1},{5,7},{7,5},{8,10},{10,8},{12,14},{14,12},{17,19},{19,... | collective-permute-start | bytes 786440 | tf_op jit(solution)/shard_map/ppermute | solution.py:304
  13.7 14.6 %copy-start.5 = (bf16[256,512]{1,0:T(8,128)(2,1)}, bf16[256,512]{1,0:T(8,128)(2,1)S(1)}, u32[]{:S(2)}) copy-start(bf16[256,512]{1,0:T(8,128)(2,1)S(1)} %broadcast_select_fusion.refs_0_) | copy-start | bytes 786436
  13.7 26.9 %collective-permute-start.10 = (bf16[256,512]{1,0:T(8,128)(2,1)S(1)}, bf16[256,512]{1,0:T(8,128)(2,1)S(1)}, u32[]{:S(2)}, u32[]{:S(2)}) collective-permute-start(bf16[256,512]{1,0:T(8,128)(2,1)S(1)} %broadcast_select_fusion.refs_0_), channel_id=1, source_target_pairs={{0,2},{1,3},{2,0},{3,1},{4,6},{5,7},{6,4},{7,5},{8,10},{9,11},{10,... | collective-permute-start | bytes 786440 | tf_op jit(solution)/shard_map/ppermute | solution.py:304
  17.6 10.7 %copy-start.7 = (bf16[256,512]{1,0:T(8,128)(2,1)}, bf16[256,512]{1,0:T(8,128)(2,1)S(1)}, u32[]{:S(2)}) copy-start(bf16[256,512]{1,0:T(8,128)(2,1)S(1)} %collective-permute-done.2.refs_1_) | copy-start | bytes 786436
  17.6 23.8 %collective-permute-start.9 = (bf16[256,512]{1,0:T(8,128)(2,1)S(1)}, bf16[256,512]{1,0:T(8,128)(2,1)S(1)}, u32[]{:S(2)}, u32[]{:S(2)}) collective-permute-start(bf16[256,512]{1,0:T(8,128)(2,1)S(1)} %collective-permute-done.2.refs_1_), channel_id=1, source_target_pairs={{0,2},{1,3},{2,0},{3,1},{4,6},{5,7},{6,4},{7,5},{8,10},{9,11},{10,... | collective-permute-start | bytes 786440 | tf_op jit(solution)/shard_map/ppermute | solution.py:304
  20.1 21.3 %copy-start.15 = (s32[16,32]{1,0:T(8,128)S(1)}, s32[16,32]{1,0:T(8,128)}, u32[]{:S(2)}) copy-start(s32[16,32]{1,0:T(8,128)} %param.15) | copy-start | bytes 6148
  28.4 17.3 %collective-permute-start.11 = (bf16[256,2048]{1,0:T(8,128)(2,1)S(1)}, bf16[256,2048]{1,0:T(8,128)(2,1)S(1)}, u32[]{:S(2)}, u32[]{:S(2)}) collective-permute-start(bf16[256,2048]{1,0:T(8,128)(2,1)S(1)} %get-tuple-element.41.refs_4_), channel_id=1, source_target_pairs={{0,1},{1,0},{2,3},{3,2},{4,5},{5,4},{6,7},{7,6},{8,9},{9,8},{10,11... | collective-permute-start | bytes 3145736 | tf_op jit(solution)/shard_map/ppermute | solution.py:312
  41.4 4.3 %collective-permute-start.12 = (bf16[256,2048]{1,0:T(8,128)(2,1)S(1)}, bf16[256,2048]{1,0:T(8,128)(2,1)S(1)}, u32[]{:S(2)}, u32[]{:S(2)}) collective-permute-start(bf16[256,2048]{1,0:T(8,128)(2,1)S(1)} %get-tuple-element.44.refs_6_), channel_id=1, source_target_pairs={{0,1},{1,0},{2,3},{3,2},{4,5},{5,4},{6,7},{7,6},{8,9},{9,8},{10,11... | collective-permute-start | bytes 3145736 | tf_op jit(solution)/shard_map/ppermute | solution.py:312
  54.9 2.9 %collective-permute-start.14 = (bf16[256,2048]{1,0:T(8,128)(2,1)S(1)}, bf16[256,2048]{1,0:T(8,128)(2,1)}, u32[]{:S(2)}, u32[]{:S(2)}) collective-permute-start(bf16[256,2048]{1,0:T(8,128)(2,1)S(1)} %get-tuple-element.49.refs_6_), channel_id=1, source_target_pairs={{0,1},{1,0},{2,3},{3,2},{4,5},{5,4},{6,7},{7,6},{8,9},{9,8},{10,11... | collective-permute-start | bytes 3145736 | tf_op jit(solution)/shard_map/ppermute | solution.py:312
  55.4 22.7 %collective-permute-start.13 = (bf16[256,512]{1,0:T(8,128)(2,1)}, bf16[256,512]{1,0:T(8,128)(2,1)S(1)}, u32[]{:S(2)}, u32[]{:S(2)}) collective-permute-start(bf16[256,512]{1,0:T(8,128)(2,1)} %get-tuple-element.46), channel_id=1, source_target_pairs={{0,2},{1,3},{2,0},{3,1},{4,6},{5,7},{6,4},{7,5},{8,10},{9,11},{10,... | collective-permute-start | bytes 786440 | tf_op jit(solution)/shard_map/ppermute | solution.py:304
  55.7 22.6 %collective-permute-start.17 = (bf16[256,512]{1,0:T(8,128)(2,1)}, bf16[256,512]{1,0:T(8,128)(2,1)S(1)}, u32[]{:S(2)}, u32[]{:S(2)}) collective-permute-start(bf16[256,512]{1,0:T(8,128)(2,1)} %get-tuple-element.59), channel_id=1, source_target_pairs={{0,2},{1,3},{2,0},{3,1},{4,6},{5,7},{6,4},{7,5},{8,10},{9,11},{10,... | collective-permute-start | bytes 786440 | tf_op jit(solution)/shard_map/ppermute | solution.py:304
  64.4 13.7 %collective-permute-start.15 = (bf16[256,512]{1,0:T(8,128)(2,1)S(1)}, bf16[256,512]{1,0:T(8,128)(2,1)S(1)}, u32[]{:S(2)}, u32[]{:S(2)}) collective-permute-start(bf16[256,512]{1,0:T(8,128)(2,1)S(1)} %get-tuple-element.53), channel_id=1, source_target_pairs={{0,2},{1,3},{2,0},{3,1},{4,6},{5,7},{6,4},{7,5},{8,10},{9,11},{10,... | collective-permute-start | bytes 786440 | tf_op jit(solution)/shard_map/ppermute | solution.py:304
  64.7 8.4 %copy-start = (bf16[256,2048]{1,0:T(8,128)(2,1)S(1)}, bf16[256,2048]{1,0:T(8,128)(2,1)}, u32[]{:S(2)}) copy-start(bf16[256,2048]{1,0:T(8,128)(2,1)} %get-tuple-element.55.left) | copy-start | bytes 3145732
  71.8 6.4 %copy-start.14 = (bf16[256,512]{1,0:T(8,128)(2,1)S(1)}, bf16[256,512]{1,0:T(8,128)(2,1)}, u32[]{:S(2)}) copy-start(bf16[256,512]{1,0:T(8,128)(2,1)} %get-tuple-element.45) | copy-start | bytes 786436
  71.8 6.5 %copy-start.13 = (bf16[256,512]{1,0:T(8,128)(2,1)S(1)}, bf16[256,512]{1,0:T(8,128)(2,1)}, u32[]{:S(2)}) copy-start(bf16[256,512]{1,0:T(8,128)(2,1)} %get-tuple-element.58) | copy-start | bytes 786436
  71.8 8.4 %collective-permute-start.20 = (bf16[256,512]{1,0:T(8,128)(2,1)S(1)}, bf16[256,512]{1,0:T(8,128)(2,1)S(1)}, u32[]{:S(2)}, u32[]{:S(2)}) collective-permute-start(bf16[256,512]{1,0:T(8,128)(2,1)S(1)} %get-tuple-element.62), channel_id=1, source_target_pairs={{0,2},{1,3},{2,0},{3,1},{4,6},{5,7},{6,4},{7,5},{8,10},{9,11},{10,... | collective-permute-start | bytes 786440 | tf_op jit(solution)/shard_map/ppermute | solution.py:304
  78.1 8.3 %copy-start.3 = (bf16[256,2048]{1,0:T(8,128)(2,1)S(1)}, bf16[256,2048]{1,0:T(8,128)(2,1)}, u32[]{:S(2)}) copy-start(bf16[256,2048]{1,0:T(8,128)(2,1)} %get-tuple-element.68.right) | copy-start | bytes 3145732
  78.1 8.3 %copy-start.4 = (bf16[256,2048]{1,0:T(8,128)(2,1)S(1)}, bf16[256,2048]{1,0:T(8,128)(2,1)}, u32[]{:S(2)}) copy-start(bf16[256,2048]{1,0:T(8,128)(2,1)} %get-tuple-element.66.left) | copy-start | bytes 3145732
  78.3 13.1 %collective-permute-start.16 = (bf16[256,512]{1,0:T(8,128)(2,1)S(1)}, bf16[256,512]{1,0:T(8,128)(2,1)S(1)}, u32[]{:S(2)}, u32[]{:S(2)}) collective-permute-start(bf16[256,512]{1,0:T(8,128)(2,1)S(1)} %add_convert_fusion.2), channel_id=1, source_target_pairs={{4,0},{12,1},{6,2},{14,3},{0,4},{8,5},{2,6},{10,7},{5,8},{13,9},{7... | collective-permute-start | bytes 786440 | tf_op jit(solution)/shard_map/ppermute | solution.py:304
  78.4 12.9 %collective-permute-start.18 = (bf16[256,512]{1,0:T(8,128)(2,1)S(1)}, bf16[256,512]{1,0:T(8,128)(2,1)S(1)}, u32[]{:S(2)}, u32[]{:S(2)}) collective-permute-start(bf16[256,512]{1,0:T(8,128)(2,1)S(1)} %add_convert_fusion.1), channel_id=1, source_target_pairs={{8,1},{10,3},{12,5},{14,7},{1,8},{3,10},{5,12},{7,14},{24,17},{26,... | collective-permute-start | bytes 786440 | tf_op jit(solution)/shard_map/ppermute | solution.py:304
  79.2 18.6 %collective-permute-start.22 = (bf16[256,512]{1,0:T(8,128)(2,1)S(1)}, bf16[256,512]{1,0:T(8,128)(2,1)S(1)}, u32[]{:S(2)}, u32[]{:S(2)}) collective-permute-start(bf16[256,512]{1,0:T(8,128)(2,1)S(1)} %add_convert_fusion.3), channel_id=1, source_target_pairs={{8,1},{10,3},{12,5},{14,7},{1,8},{3,10},{5,12},{7,14},{24,17},{26,... | collective-permute-start | bytes 786440 | tf_op jit(solution)/shard_map/ppermute | solution.py:304
  85.3 12.5 %collective-permute-start.21 = (bf16[256,512]{1,0:T(8,128)(2,1)S(1)}, bf16[256,512]{1,0:T(8,128)(2,1)S(1)}, u32[]{:S(2)}, u32[]{:S(2)}) collective-permute-start(bf16[256,512]{1,0:T(8,128)(2,1)S(1)} %add_convert_fusion), channel_id=1, source_target_pairs={{4,0},{12,1},{6,2},{14,3},{0,4},{8,5},{2,6},{10,7},{5,8},{13,9},{7... | collective-permute-start | bytes 786440 | tf_op jit(solution)/shard_map/ppermute | solution.py:304
  91.5 13.1 %collective-permute-start.19 = (bf16[128,512]{1,0:T(8,128)(2,1)S(1)}, bf16[128,512]{1,0:T(8,128)(2,1)S(1)}, u32[]{:S(2)}, u32[]{:S(2)}) collective-permute-start(bf16[128,512]{1,0:T(8,128)(2,1)S(1)} %dynamic-slice_convert_fusion.1), channel_id=1, source_target_pairs={{0,1},{1,0},{2,3},{3,2},{4,5},{5,4},{6,7},{7,6},{8,9},{9,8},{10,11... | collective-permute-start | bytes 393224 | tf_op jit(solution)/shard_map/ppermute | solution.py:312
  98.0 7.6 %collective-permute-start.23 = (bf16[128,512]{1,0:T(8,128)(2,1)S(1)}, bf16[128,512]{1,0:T(8,128)(2,1)S(1)}, u32[]{:S(2)}, u32[]{:S(2)}) collective-permute-start(bf16[128,512]{1,0:T(8,128)(2,1)S(1)} %dynamic-slice_convert_fusion), channel_id=1, source_target_pairs={{0,1},{1,0},{2,3},{3,2},{4,5},{5,4},{6,7},{7,6},{8,9},{9,8},{10,11... | collective-permute-start | bytes 393224 | tf_op jit(solution)/shard_map/ppermute | solution.py:312
  (8 other events, 21.1 us)
where the time goes:
time: 107 us; the launch traced here: 106 us
  Pallas kernels  46.1 us (43%)
  starting transfers between devices  42.4 us (40%)
  waiting for transfers between devices  6.84 us (6%)
  local copies, waits for them, and re-layouts  5.1 us (5%)
  other arithmetic  4.72 us (4%)
    pallas_call x4, Pallas kernels, call(): pl.pallas_call(body, grid=(1,), in_specs=[pl.BlockSpec(memory_space=pltpu...  27.2 us
    ppermute x7, starting transfers between devices, swap(): return lax.ppermute(part, 'dp', [(0, 1), (1, 0)])  27 us
    ppermute x17, starting transfers between devices, permute(): return lax.ppermute(x, ('tp', 'dp'), route)  15.5 us
    pallas_call x3, Pallas kernels, weight_grad(): pl.pallas_call(weight_grad_body, grid=(height // tile,), in_specs=[pl.Blo...  14.9 us
    unnamed x32, local copies, waits for them, and re-layouts  4.63 us
    ppermute x17, waiting for transfers between devices, permute(): return lax.ppermute(x, ('tp', 'dp'), route)  4.39 us
    pallas_call x1, Pallas kernels, prepare(): pl.pallas_call(prepare_body, grid=(rows // tile,), in_specs=[pl.BlockSpec...  4 us
    ppermute x7, waiting for transfers between devices, swap(): return lax.ppermute(part, 'dp', [(0, 1), (1, 0)])  2.46 us
  transfers between devices with their start and end apart: 24, of which 6 were waited for; matrix products, arithmetic and copies ran while one was open for 3% of the time, Pallas kernels for 37%

commit v1 on v0

--- a/solution.py
+++ b/solution.py
@@ -192,11 +192,12 @@
         sel,
         [],
         [w_down],
-        [*blocks, *sums],
+        [*[in_hbm(block) for block in blocks], *sums],
         shapes(rows, width, BF16)
         + late(rows, depth)
         + late(rows, width)
-        + shapes(rows, width, F32, F32)
+        + shapes(rows, width, F32)
+        + [pltpu.HBM((rows, width), F32)]
         + late(rows, depth // half) * half,
         [],
         4 * rows * depth * width,
@@ -456,7 +457,7 @@
     grad, cot, hidden, by_gate, by_up, *out_blocks = middle(
         sel, cot_blocks, sums, w_held, half, rows
     )
-    deltas = [by_gate, by_up, grad, swap(grad)]
+    deltas = [by_gate, in_hbm(by_up), grad, swap(grad)]
     gate_up = lambda wanted, make, arrays, name: product(
         sel, wanted, make, arrays, [w_gate, w_up], [keep_gate, keep_up], half, name
     )

time: 107 us -> 104 us (0.972)
  local copies, waits for them, and re-layouts: 5.1 us -> 1.1 us
  Pallas kernels: 46.1 us -> 47.8 us
    unnamed x32 -> x20, local copies, waits for them, and re-layouts: 4.63 us -> 0.63 us
    pallas_call x4, Pallas kernels: 27.2 us -> 28.9 us  [call(): pl.pallas_call(body, grid=(1,), in_specs=[pl.BlockSpec(memory_space=pltpu...]
  transfers between devices with their start and end apart: 24 -> 24, of which waited for: 6 -> 6; matrix products, arithmetic and copies ran while one was open for 3% -> 3% of each run, Pallas kernels for 37% -> 38%
where the time goes in v1:
time: 104 us
  Pallas kernels  47.8 us (46%)
  starting transfers between devices  41.6 us (40%)
  waiting for transfers between devices  7.42 us (7%)
  other arithmetic  4.72 us (5%)
  local copies, waits for them, and re-layouts  1.1 us (1%)
    pallas_call x4, Pallas kernels, call(): pl.pallas_call(body, grid=(1,), in_specs=[pl.BlockSpec(memory_space=pltpu...  28.9 us
    ppermute x7, starting transfers between devices, swap(): return lax.ppermute(part, 'dp', [(0, 1), (1, 0)])  26.4 us
    ppermute x17, starting transfers between devices, permute(): return lax.ppermute(x, ('tp', 'dp'), route)  15.3 us
    pallas_call x3, Pallas kernels, weight_grad(): pl.pallas_call(weight_grad_body, grid=(height // tile,), in_specs=[pl.Blo...  14.9 us
    ppermute x17, waiting for transfers between devices, permute(): return lax.ppermute(x, ('tp', 'dp'), route)  4.61 us
    pallas_call x1, Pallas kernels, prepare(): pl.pallas_call(prepare_body, grid=(rows // tile,), in_specs=[pl.BlockSpec...  3.98 us
    ppermute x7, waiting for transfers between devices, swap(): return lax.ppermute(part, 'dp', [(0, 1), (1, 0)])  2.81 us
  transfers between devices with their start and end apart: 24, of which 6 were waited for; matrix products, arithmetic and copies ran while one was open for 3% of the time, Pallas kernels for 38%

profile of v1, /device:TPU:19, one launch (start us, length us, event | category | flops | bytes accessed | tf_op | source)
XLA Modules:
  0.0 103.6 jit_solution(11319193929167954032)
XLA Ops:
  0.6 0.7 collective-permute-start
  1.4 1.2 %collective-permute-done = bf16[128,512]{1,0:T(8,128)(2,1)S(1)} collective-permute-done((bf16[128,512]{1,0:T(8,128)(2,1)}, bf16[128,512]{1,0:T(8,128)(2,1)S(1)}, u32[]{:S(2)}, u32[]{:S(2)}) %collective-permute-start) | collective-permute-done | bytes 131104 | tf_op jit(solution)/shard_map/ppermute | solution.py:313
  2.6 0.9 broadcast_select_fusion.4
  4.0 1.3 %collective-permute-start.5 = (bf16[256,512]{1,0:T(8,128)(2,1)S(1)}, bf16[256,512]{1,0:T(8,128)(2,1)S(1)}, u32[]{:S(2)}, u32[]{:S(2)}) collective-permute-start(bf16[256,512]{1,0:T(8,128)(2,1)S(1)} %pad_maximum_fusion.refs_0_), channel_id=1, source_target_pairs={{0,4},{1,12},{2,6},{3,14},{4,0},{5,8},{6,2},{7,10},{8,5},{9,13},{1... | collective-permute-start | bytes 786440 | tf_op jit(solution)/shard_map/ppermute | solution.py:305
  5.2 0.7 collective-permute-start.4
  5.9 0.9 broadcast_select_fusion.2
  6.9 0.7 collective-permute-start.3
  8.2 3.1 %collective-permute-start.6 = (bf16[256,512]{1,0:T(8,128)(2,1)S(1)}, bf16[256,512]{1,0:T(8,128)(2,1)S(1)}, u32[]{:S(2)}, u32[]{:S(2)}) collective-permute-start(bf16[256,512]{1,0:T(8,128)(2,1)S(1)} %pad_maximum_fusion.refs_0_), channel_id=1, source_target_pairs={{0,2},{2,0},{4,6},{6,4},{9,11},{11,9},{13,15},{15,13},{16,18},{18,... | collective-permute-start | bytes 786440 | tf_op jit(solution)/shard_map/ppermute | solution.py:305
  11.7 1.2 %collective-permute-start.7 = (bf16[256,512]{1,0:T(8,128)(2,1)S(1)}, bf16[256,512]{1,0:T(8,128)(2,1)S(1)}, u32[]{:S(2)}, u32[]{:S(2)}) collective-permute-start(bf16[256,512]{1,0:T(8,128)(2,1)S(1)} %collective-permute-done.5.refs_2_), channel_id=1, source_target_pairs={{0,2},{1,3},{2,0},{3,1},{4,6},{5,7},{6,4},{7,5},{8,10},{9,11},{10,... | collective-permute-start | bytes 786440 | tf_op jit(solution)/shard_map/ppermute | solution.py:305
  13.0 0.7 collective-permute-start.8
  14.0 3.6 %collective-permute-done.2.refs_1_ = bf16[256,512]{1,0:T(8,128)(2,1)S(1)} collective-permute-done((bf16[256,512]{1,0:T(8,128)(2,1)S(1)}, bf16[256,512]{1,0:T(8,128)(2,1)S(1)}, u32[]{:S(2)}, u32[]{:S(2)}) %collective-permute-start.2) | collective-permute-done | bytes 262176 | tf_op jit(solution)/shard_map/ppermute | solution.py:305
  17.6 1.2 %collective-permute-start.9 = (bf16[256,512]{1,0:T(8,128)(2,1)S(1)}, bf16[256,512]{1,0:T(8,128)(2,1)S(1)}, u32[]{:S(2)}, u32[]{:S(2)}) collective-permute-start(bf16[256,512]{1,0:T(8,128)(2,1)S(1)} %collective-permute-done.2.refs_1_), channel_id=1, source_target_pairs={{0,2},{1,3},{2,0},{3,1},{4,6},{5,7},{6,4},{7,5},{8,10},{9,11},{10,... | collective-permute-start | bytes 786440 | tf_op jit(solution)/shard_map/ppermute | solution.py:305
  18.9 0.8 dynamic-slice_convert_fusion.2
  20.1 8.2 %forward.1 = (bf16[256,2048]{1,0:T(8,128)(2,1)S(1)}, bf16[256,2048]{1,0:T(8,128)(2,1)S(1)}, bf16[256,2048]{1,0:T(8,128)(2,1)}) custom-call(s32[2]{0:T(128)S(1)} %pad_add_fusion.sel, bf16[2048,2048]{1,0:T(8,128)(2,1)} %refs_0_.3, bf16[2048,2048]{1,0:T(8,128)(2,1)} %refs_1_.3, f32[16,1,2048]{2,1,0:T(1,128)S(1)} %bitcast.9, f32[16,1,2048]{2,1,0:T(1,128)S(1)} %bitcast.5, ...), custom_call_target="tpu_custom_call" | custom-call | flops 67108864 | bytes 262144 | tf_op jit(solution)/shard_map/forward/pallas_call | solution.py:36
  28.4 12.3 %collective-permute-start.11 = (bf16[256,2048]{1,0:T(8,128)(2,1)S(1)}, bf16[256,2048]{1,0:T(8,128)(2,1)S(1)}, u32[]{:S(2)}, u32[]{:S(2)}) collective-permute-start(bf16[256,2048]{1,0:T(8,128)(2,1)S(1)} %get-tuple-element.41.refs_4_), channel_id=1, source_target_pairs={{0,1},{1,0},{2,3},{3,2},{4,5},{5,4},{6,7},{7,6},{8,9},{9,8},{10,11... | collective-permute-start | bytes 3145736 | tf_op jit(solution)/shard_map/ppermute | solution.py:313
  41.6 4.0 %prepare_down.1.weight = bf16[2048,2048]{1,0:T(8,128)(2,1)S(1)} custom-call(bf16[2048,2048]{1,0:T(8,128)(2,1)} %weight.1, f32[16,1,2048]{2,1,0:T(1,128)S(1)} %bitcast.13), custom_call_target="tpu_custom_call" | custom-call | bytes 262144 | tf_op jit(solution)/shard_map/prepare_down/pallas_call | solution.py:66
  45.6 8.0 %middle.1 = (bf16[256,2048]{1,0:T(8,128)(2,1)S(1)}, bf16[256,2048]{1,0:T(8,128)(2,1)}, bf16[256,2048]{1,0:T(8,128)(2,1)}, f32[256,2048]{1,0:T(8,128)S(1)}, f32[2...) custom-call(s32[2]{0:T(128)S(1)} %pad_add_fusion.sel, ...), custom_call_target="tpu_custom_call" | custom-call | flops 4294967296 | bytes 16777216 | tf_op jit(solution)/shard_map/middle/pallas_call | solution.py:36
  53.9 1.2 %collective-permute-start.17 = (bf16[256,512]{1,0:T(8,128)(2,1)}, bf16[256,512]{1,0:T(8,128)(2,1)S(1)}, u32[]{:S(2)}, u32[]{:S(2)}) collective-permute-start(bf16[256,512]{1,0:T(8,128)(2,1)} %get-tuple-element.59), channel_id=1, source_target_pairs={{0,2},{1,3},{2,0},{3,1},{4,6},{5,7},{6,4},{7,5},{8,10},{9,11},{10,... | collective-permute-start | bytes 786440 | tf_op jit(solution)/shard_map/ppermute | solution.py:305
  55.1 1.3 %collective-permute-done.14.refs_7_ = bf16[256,2048]{1,0:T(8,128)(2,1)} collective-permute-done((bf16[256,2048]{1,0:T(8,128)(2,1)S(1)}, bf16[256,2048]{1,0:T(8,128)(2,1)}, u32[]{:S(2)}, u32[]{:S(2)}) %collective-permute-start.14) | collective-permute-done | bytes 1048608 | tf_op jit(solution)/shard_map/ppermute | solution.py:313
  56.4 5.5 %input_first.1 = (bf16[256,512]{1,0:T(8,128)(2,1)S(1)}, bf16[256,2048]{1,0:T(8,128)(2,1)S(1)}, bf16[256,2048]{1,0:T(8,128)(2,1)S(1)}) custom-call(s32[2]{0:T(128)S(1)} %pad_add_fusion.sel, bf16[2048,2048]{1,0:T(8,128)(2,1)} %refs_0_.3, bf16[2048,2048]{1,0:T(8,128)(2,1)} %refs_1_.3, f32[16,1,2048]{2,1,0:T(1,128)S(1)} %bitcast.10, f32[16,1,2048]{2,1,0:T(1,128)S(1)} %bitcast.6, ...), custom_call_target="tpu_custom_call" | custom-call | flops 1073741824 | bytes 4194304 | tf_op jit(solution)/shard_map/input_first/pallas_call | solution.py:36
  62.2 7.1 %input_rest.1 = (bf16[256,512]{1,0:T(8,128)(2,1)S(1)}, bf16[256,512]{1,0:T(8,128)(2,1)S(1)}, bf16[256,512]{1,0:T(8,128)(2,1)S(1)}) custom-call(s32[2]{0:T(128)S(1)} %pad_add_fusion.sel, bf16[2048,2048]{1,0:T(8,128)(2,1)} %refs_0_.3, bf16[2048,2048]{1,0:T(8,128)(2,1)} %refs_1_.3, f32[16,1,2048]{2,1,0:T(1,128)S(1)} %bitcast.11, f32[16,1,2048]{2,1,0:T(1,128)S(1)} %bitcast.7, ...), custom_call_target="tpu_custom_call" | custom-call | flops 3221225472 | bytes 12582912 | tf_op jit(solution)/shard_map/input_rest/pallas_call | solution.py:36
  69.4 1.3 %collective-permute-start.20 = (bf16[256,512]{1,0:T(8,128)(2,1)S(1)}, bf16[256,512]{1,0:T(8,128)(2,1)S(1)}, u32[]{:S(2)}, u32[]{:S(2)}) collective-permute-start(bf16[256,512]{1,0:T(8,128)(2,1)S(1)} %get-tuple-element.62), channel_id=1, source_target_pairs={{0,2},{1,3},{2,0},{3,1},{4,6},{5,7},{6,4},{7,5},{8,10},{9,11},{10,... | collective-permute-start | bytes 786440 | tf_op jit(solution)/shard_map/ppermute | solution.py:305
  70.7 5.0 %gate_grad.1 = bf16[2048,2048]{1,0:T(8,128)(2,1)} custom-call(bf16[256,2048]{1,0:T(8,128)(2,1)S(1)} %copy-done, bf16[256,2048]{1,0:T(8,128)(2,1)S(1)} %get-tuple-element.50.refs_4_.right, f32[16,1,2048]{2,1,0:T(1,128)S(1)} %bitcast.12), custom_call_target="tpu_custom_call" | custom-call | flops 2147483648 | bytes 8388608 | tf_op jit(solution)/shard_map/gate_grad/pallas_call | solution.py:282
  76.0 0.8 collective-permute-start.18
  76.8 0.7 collective-permute-start.22
  78.1 5.0 %up_grad.1 = bf16[2048,2048]{1,0:T(8,128)(2,1)} custom-call(bf16[256,2048]{1,0:T(8,128)(2,1)S(1)} %copy-done, bf16[256,2048]{1,0:T(8,128)(2,1)S(1)} %get-tuple-element.64.refs_5_.right, f32[16,1,2048]{2,1,0:T(1,128)S(1)} %bitcast.8), custom_call_target="tpu_custom_call" | custom-call | flops 2147483648 | bytes 8388608 | tf_op jit(solution)/shard_map/up_grad/pallas_call | solution.py:282
  83.1 0.8 collective-permute-start.21
  84.0 4.9 %down_grad.1 = bf16[2048,2048]{1,0:T(8,128)(2,1)} custom-call(bf16[256,2048]{1,0:T(8,128)(2,1)S(1)} %copy-done.2, bf16[256,2048]{1,0:T(8,128)(2,1)S(1)} %copy-done.1, f32[16,1,2048]{2,1,0:T(1,128)S(1)} %bitcast.14), custom_call_target="tpu_custom_call" | custom-call | flops 2147483648 | bytes 8388608 | tf_op jit(solution)/shard_map/down_grad/pallas_call | solution.py:282
  89.0 6.2 %collective-permute-start.19 = (bf16[128,512]{1,0:T(8,128)(2,1)S(1)}, bf16[128,512]{1,0:T(8,128)(2,1)S(1)}, u32[]{:S(2)}, u32[]{:S(2)}) collective-permute-start(bf16[128,512]{1,0:T(8,128)(2,1)S(1)} %dynamic-slice_convert_fusion.1), channel_id=1, source_target_pairs={{0,1},{1,0},{2,3},{3,2},{4,5},{5,4},{6,7},{7,6},{8,9},{9,8},{10,11... | collective-permute-start | bytes 393224 | tf_op jit(solution)/shard_map/ppermute | solution.py:313
  95.3 6.6 %collective-permute-start.23 = (bf16[128,512]{1,0:T(8,128)(2,1)S(1)}, bf16[128,512]{1,0:T(8,128)(2,1)S(1)}, u32[]{:S(2)}, u32[]{:S(2)}) collective-permute-start(bf16[128,512]{1,0:T(8,128)(2,1)S(1)} %dynamic-slice_convert_fusion), channel_id=1, source_target_pairs={{0,1},{1,0},{2,3},{3,2},{4,5},{5,4},{6,7},{7,6},{8,9},{9,8},{10,11... | collective-permute-start | bytes 393224 | tf_op jit(solution)/shard_map/ppermute | solution.py:313
  101.9 0.7 add_convert_fusion.5
  102.9 0.7 add_convert_fusion.4
  (67 shorter events, 5.2 us)
Async XLA Ops:
  0.6 1.9 %collective-permute-start = (bf16[128,512]{1,0:T(8,128)(2,1)}, bf16[128,512]{1,0:T(8,128)(2,1)S(1)}, u32[]{:S(2)}, u32[]{:S(2)}) collective-permute-start(bf16[128,512]{1,0:T(8,128)(2,1)} %param.8), channel_id=1, source_target_pairs={{0,1},{1,0},{2,3},{3,2},{4,5},{5,4},{6,7},{7,6},{8,9},{9,8},{10,11... | collective-permute-start | bytes 393224 | tf_op jit(solution)/shard_map/ppermute | solution.py:313
  3.5 2.4 %collective-permute-start.1 = (bf16[128,512]{1,0:T(8,128)(2,1)}, bf16[128,512]{1,0:T(8,128)(2,1)S(1)}, u32[]{:S(2)}, u32[]{:S(2)}) collective-permute-start(bf16[128,512]{1,0:T(8,128)(2,1)} %param.9), channel_id=1, source_target_pairs={{0,1},{1,0},{2,3},{3,2},{4,5},{5,4},{6,7},{7,6},{8,9},{9,8},{10,11... | collective-permute-start | bytes 393224 | tf_op jit(solution)/shard_map/ppermute | solution.py:313
  4.0 7.8 %collective-permute-start.5 = (bf16[256,512]{1,0:T(8,128)(2,1)S(1)}, bf16[256,512]{1,0:T(8,128)(2,1)S(1)}, u32[]{:S(2)}, u32[]{:S(2)}) collective-permute-start(bf16[256,512]{1,0:T(8,128)(2,1)S(1)} %pad_maximum_fusion.refs_0_), channel_id=1, source_target_pairs={{0,4},{1,12},{2,6},{3,14},{4,0},{5,8},{6,2},{7,10},{8,5},{9,13},{1... | collective-permute-start | bytes 786440 | tf_op jit(solution)/shard_map/ppermute | solution.py:305
  5.2 7.7 %collective-permute-start.4 = (bf16[256,512]{1,0:T(8,128)(2,1)S(1)}, bf16[256,512]{1,0:T(8,128)(2,1)S(1)}, u32[]{:S(2)}, u32[]{:S(2)}) collective-permute-start(bf16[256,512]{1,0:T(8,128)(2,1)S(1)} %pad_maximum_fusion.refs_0_), channel_id=1, source_target_pairs={{1,8},{3,10},{5,12},{7,14},{8,1},{10,3},{12,5},{14,7},{17,24},{19,... | collective-permute-start | bytes 786440 | tf_op jit(solution)/shard_map/ppermute | solution.py:305
  6.9 6.7 %collective-permute-start.3 = (bf16[256,512]{1,0:T(8,128)(2,1)S(1)}, bf16[256,512]{1,0:T(8,128)(2,1)S(1)}, u32[]{:S(2)}, u32[]{:S(2)}) collective-permute-start(bf16[256,512]{1,0:T(8,128)(2,1)S(1)} %pad_maximum_fusion.1), channel_id=1, source_target_pairs={{1,8},{3,10},{5,12},{7,14},{8,1},{10,3},{12,5},{14,7},{17,24},{19,... | collective-permute-start | bytes 786440 | tf_op jit(solution)/shard_map/ppermute | solution.py:305
  7.6 10.1 %collective-permute-start.2 = (bf16[256,512]{1,0:T(8,128)(2,1)S(1)}, bf16[256,512]{1,0:T(8,128)(2,1)S(1)}, u32[]{:S(2)}, u32[]{:S(2)}) collective-permute-start(bf16[256,512]{1,0:T(8,128)(2,1)S(1)} %pad_maximum_fusion.1), channel_id=1, source_target_pairs={{0,4},{1,12},{2,6},{3,14},{4,0},{5,8},{6,2},{7,10},{8,5},{9,13},{1... | collective-permute-start | bytes 786440 | tf_op jit(solution)/shard_map/ppermute | solution.py:305
  8.2 11.7 %collective-permute-start.6 = (bf16[256,512]{1,0:T(8,128)(2,1)S(1)}, bf16[256,512]{1,0:T(8,128)(2,1)S(1)}, u32[]{:S(2)}, u32[]{:S(2)}) collective-permute-start(bf16[256,512]{1,0:T(8,128)(2,1)S(1)} %pad_maximum_fusion.refs_0_), channel_id=1, source_target_pairs={{0,2},{2,0},{4,6},{6,4},{9,11},{11,9},{13,15},{15,13},{16,18},{18,... | collective-permute-start | bytes 786440 | tf_op jit(solution)/shard_map/ppermute | solution.py:305
  11.7 8.2 %collective-permute-start.7 = (bf16[256,512]{1,0:T(8,128)(2,1)S(1)}, bf16[256,512]{1,0:T(8,128)(2,1)S(1)}, u32[]{:S(2)}, u32[]{:S(2)}) collective-permute-start(bf16[256,512]{1,0:T(8,128)(2,1)S(1)} %collective-permute-done.5.refs_2_), channel_id=1, source_target_pairs={{0,2},{1,3},{2,0},{3,1},{4,6},{5,7},{6,4},{7,5},{8,10},{9,11},{10,... | collective-permute-start | bytes 786440 | tf_op jit(solution)/shard_map/ppermute | solution.py:305
  13.0 6.9 %collective-permute-start.8 = (bf16[256,512]{1,0:T(8,128)(2,1)S(1)}, bf16[256,512]{1,0:T(8,128)(2,1)S(1)}, u32[]{:S(2)}, u32[]{:S(2)}) collective-permute-start(bf16[256,512]{1,0:T(8,128)(2,1)S(1)} %collective-permute-done.4.refs_1_), channel_id=1, source_target_pairs={{1,3},{3,1},{5,7},{7,5},{8,10},{10,8},{12,14},{14,12},{17,19},{19,... | collective-permute-start | bytes 786440 | tf_op jit(solution)/shard_map/ppermute | solution.py:305
  13.7 14.6 %copy-start.5 = (bf16[256,512]{1,0:T(8,128)(2,1)}, bf16[256,512]{1,0:T(8,128)(2,1)S(1)}, u32[]{:S(2)}) copy-start(bf16[256,512]{1,0:T(8,128)(2,1)S(1)} %broadcast_select_fusion.refs_0_) | copy-start | bytes 786436
  13.7 26.9 %collective-permute-start.10 = (bf16[256,512]{1,0:T(8,128)(2,1)S(1)}, bf16[256,512]{1,0:T(8,128)(2,1)S(1)}, u32[]{:S(2)}, u32[]{:S(2)}) collective-permute-start(bf16[256,512]{1,0:T(8,128)(2,1)S(1)} %broadcast_select_fusion.refs_0_), channel_id=1, source_target_pairs={{0,2},{1,3},{2,0},{3,1},{4,6},{5,7},{6,4},{7,5},{8,10},{9,11},{10,... | collective-permute-start | bytes 786440 | tf_op jit(solution)/shard_map/ppermute | solution.py:305
  17.6 10.7 %copy-start.7 = (bf16[256,512]{1,0:T(8,128)(2,1)}, bf16[256,512]{1,0:T(8,128)(2,1)S(1)}, u32[]{:S(2)}) copy-start(bf16[256,512]{1,0:T(8,128)(2,1)S(1)} %collective-permute-done.2.refs_1_) | copy-start | bytes 786436
  17.6 23.0 %collective-permute-start.9 = (bf16[256,512]{1,0:T(8,128)(2,1)S(1)}, bf16[256,512]{1,0:T(8,128)(2,1)S(1)}, u32[]{:S(2)}, u32[]{:S(2)}) collective-permute-start(bf16[256,512]{1,0:T(8,128)(2,1)S(1)} %collective-permute-done.2.refs_1_), channel_id=1, source_target_pairs={{0,2},{1,3},{2,0},{3,1},{4,6},{5,7},{6,4},{7,5},{8,10},{9,11},{10,... | collective-permute-start | bytes 786440 | tf_op jit(solution)/shard_map/ppermute | solution.py:305
  20.1 21.3 %copy-start.6 = (s32[16,32]{1,0:T(8,128)S(1)}, s32[16,32]{1,0:T(8,128)}, u32[]{:S(2)}) copy-start(s32[16,32]{1,0:T(8,128)} %param.15) | copy-start | bytes 6148
  28.4 17.2 %collective-permute-start.11 = (bf16[256,2048]{1,0:T(8,128)(2,1)S(1)}, bf16[256,2048]{1,0:T(8,128)(2,1)S(1)}, u32[]{:S(2)}, u32[]{:S(2)}) collective-permute-start(bf16[256,2048]{1,0:T(8,128)(2,1)S(1)} %get-tuple-element.41.refs_4_), channel_id=1, source_target_pairs={{0,1},{1,0},{2,3},{3,2},{4,5},{5,4},{6,7},{7,6},{8,9},{9,8},{10,11... | collective-permute-start | bytes 3145736 | tf_op jit(solution)/shard_map/ppermute | solution.py:313
  40.7 4.9 %collective-permute-start.12 = (bf16[256,2048]{1,0:T(8,128)(2,1)S(1)}, bf16[256,2048]{1,0:T(8,128)(2,1)S(1)}, u32[]{:S(2)}, u32[]{:S(2)}) collective-permute-start(bf16[256,2048]{1,0:T(8,128)(2,1)S(1)} %get-tuple-element.44.refs_6_), channel_id=1, source_target_pairs={{0,1},{1,0},{2,3},{3,2},{4,5},{5,4},{6,7},{7,6},{8,9},{9,8},{10,11... | collective-permute-start | bytes 3145736 | tf_op jit(solution)/shard_map/ppermute | solution.py:313
  53.6 2.8 %collective-permute-start.14 = (bf16[256,2048]{1,0:T(8,128)(2,1)S(1)}, bf16[256,2048]{1,0:T(8,128)(2,1)}, u32[]{:S(2)}, u32[]{:S(2)}) collective-permute-start(bf16[256,2048]{1,0:T(8,128)(2,1)S(1)} %get-tuple-element.49.refs_6_), channel_id=1, source_target_pairs={{0,1},{1,0},{2,3},{3,2},{4,5},{5,4},{6,7},{7,6},{8,9},{9,8},{10,11... | collective-permute-start | bytes 3145736 | tf_op jit(solution)/shard_map/ppermute | solution.py:313
  53.6 22.1 %collective-permute-start.13 = (bf16[256,512]{1,0:T(8,128)(2,1)}, bf16[256,512]{1,0:T(8,128)(2,1)S(1)}, u32[]{:S(2)}, u32[]{:S(2)}) collective-permute-start(bf16[256,512]{1,0:T(8,128)(2,1)} %get-tuple-element.46), channel_id=1, source_target_pairs={{0,2},{1,3},{2,0},{3,1},{4,6},{5,7},{6,4},{7,5},{8,10},{9,11},{10,... | collective-permute-start | bytes 786440 | tf_op jit(solution)/shard_map/ppermute | solution.py:305
  53.9 22.0 %collective-permute-start.17 = (bf16[256,512]{1,0:T(8,128)(2,1)}, bf16[256,512]{1,0:T(8,128)(2,1)S(1)}, u32[]{:S(2)}, u32[]{:S(2)}) collective-permute-start(bf16[256,512]{1,0:T(8,128)(2,1)} %get-tuple-element.59), channel_id=1, source_target_pairs={{0,2},{1,3},{2,0},{3,1},{4,6},{5,7},{6,4},{7,5},{8,10},{9,11},{10,... | collective-permute-start | bytes 786440 | tf_op jit(solution)/shard_map/ppermute | solution.py:305
  61.9 13.7 %collective-permute-start.15 = (bf16[256,512]{1,0:T(8,128)(2,1)S(1)}, bf16[256,512]{1,0:T(8,128)(2,1)S(1)}, u32[]{:S(2)}, u32[]{:S(2)}) collective-permute-start(bf16[256,512]{1,0:T(8,128)(2,1)S(1)} %get-tuple-element.53), channel_id=1, source_target_pairs={{0,2},{1,3},{2,0},{3,1},{4,6},{5,7},{6,4},{7,5},{8,10},{9,11},{10,... | collective-permute-start | bytes 786440 | tf_op jit(solution)/shard_map/ppermute | solution.py:305
  62.2 8.4 %copy-start = (bf16[256,2048]{1,0:T(8,128)(2,1)S(1)}, bf16[256,2048]{1,0:T(8,128)(2,1)}, u32[]{:S(2)}) copy-start(bf16[256,2048]{1,0:T(8,128)(2,1)} %get-tuple-element.55.left) | copy-start | bytes 3145732
  69.4 6.4 %copy-start.4 = (bf16[256,512]{1,0:T(8,128)(2,1)S(1)}, bf16[256,512]{1,0:T(8,128)(2,1)}, u32[]{:S(2)}) copy-start(bf16[256,512]{1,0:T(8,128)(2,1)} %get-tuple-element.45) | copy-start | bytes 786436
  69.4 6.5 %copy-start.3 = (bf16[256,512]{1,0:T(8,128)(2,1)S(1)}, bf16[256,512]{1,0:T(8,128)(2,1)}, u32[]{:S(2)}) copy-start(bf16[256,512]{1,0:T(8,128)(2,1)} %get-tuple-element.58) | copy-start | bytes 786436
  69.4 8.7 %collective-permute-start.20 = (bf16[256,512]{1,0:T(8,128)(2,1)S(1)}, bf16[256,512]{1,0:T(8,128)(2,1)S(1)}, u32[]{:S(2)}, u32[]{:S(2)}) collective-permute-start(bf16[256,512]{1,0:T(8,128)(2,1)S(1)} %get-tuple-element.62), channel_id=1, source_target_pairs={{0,2},{1,3},{2,0},{3,1},{4,6},{5,7},{6,4},{7,5},{8,10},{9,11},{10,... | collective-permute-start | bytes 786440 | tf_op jit(solution)/shard_map/ppermute | solution.py:305
  75.7 8.3 %copy-start.1 = (bf16[256,2048]{1,0:T(8,128)(2,1)S(1)}, bf16[256,2048]{1,0:T(8,128)(2,1)}, u32[]{:S(2)}) copy-start(bf16[256,2048]{1,0:T(8,128)(2,1)} %get-tuple-element.68.right) | copy-start | bytes 3145732
  75.7 8.3 %copy-start.2 = (bf16[256,2048]{1,0:T(8,128)(2,1)S(1)}, bf16[256,2048]{1,0:T(8,128)(2,1)}, u32[]{:S(2)}) copy-start(bf16[256,2048]{1,0:T(8,128)(2,1)} %get-tuple-element.66.left) | copy-start | bytes 3145732
  75.9 13.1 %collective-permute-start.16 = (bf16[256,512]{1,0:T(8,128)(2,1)S(1)}, bf16[256,512]{1,0:T(8,128)(2,1)S(1)}, u32[]{:S(2)}, u32[]{:S(2)}) collective-permute-start(bf16[256,512]{1,0:T(8,128)(2,1)S(1)} %add_convert_fusion.2), channel_id=1, source_target_pairs={{4,0},{12,1},{6,2},{14,3},{0,4},{8,5},{2,6},{10,7},{5,8},{13,9},{7... | collective-permute-start | bytes 786440 | tf_op jit(solution)/shard_map/ppermute | solution.py:305
  76.0 12.9 %collective-permute-start.18 = (bf16[256,512]{1,0:T(8,128)(2,1)S(1)}, bf16[256,512]{1,0:T(8,128)(2,1)S(1)}, u32[]{:S(2)}, u32[]{:S(2)}) collective-permute-start(bf16[256,512]{1,0:T(8,128)(2,1)S(1)} %add_convert_fusion.1), channel_id=1, source_target_pairs={{8,1},{10,3},{12,5},{14,7},{1,8},{3,10},{5,12},{7,14},{24,17},{26,... | collective-permute-start | bytes 786440 | tf_op jit(solution)/shard_map/ppermute | solution.py:305
  76.8 18.4 %collective-permute-start.22 = (bf16[256,512]{1,0:T(8,128)(2,1)S(1)}, bf16[256,512]{1,0:T(8,128)(2,1)S(1)}, u32[]{:S(2)}, u32[]{:S(2)}) collective-permute-start(bf16[256,512]{1,0:T(8,128)(2,1)S(1)} %add_convert_fusion.3), channel_id=1, source_target_pairs={{8,1},{10,3},{12,5},{14,7},{1,8},{3,10},{5,12},{7,14},{24,17},{26,... | collective-permute-start | bytes 786440 | tf_op jit(solution)/shard_map/ppermute | solution.py:305
  83.1 12.1 %collective-permute-start.21 = (bf16[256,512]{1,0:T(8,128)(2,1)S(1)}, bf16[256,512]{1,0:T(8,128)(2,1)S(1)}, u32[]{:S(2)}, u32[]{:S(2)}) collective-permute-start(bf16[256,512]{1,0:T(8,128)(2,1)S(1)} %add_convert_fusion), channel_id=1, source_target_pairs={{4,0},{12,1},{6,2},{14,3},{0,4},{8,5},{2,6},{10,7},{5,8},{13,9},{7... | collective-permute-start | bytes 786440 | tf_op jit(solution)/shard_map/ppermute | solution.py:305
  89.0 12.9 %collective-permute-start.19 = (bf16[128,512]{1,0:T(8,128)(2,1)S(1)}, bf16[128,512]{1,0:T(8,128)(2,1)S(1)}, u32[]{:S(2)}, u32[]{:S(2)}) collective-permute-start(bf16[128,512]{1,0:T(8,128)(2,1)S(1)} %dynamic-slice_convert_fusion.1), channel_id=1, source_target_pairs={{0,1},{1,0},{2,3},{3,2},{4,5},{5,4},{6,7},{7,6},{8,9},{9,8},{10,11... | collective-permute-start | bytes 393224 | tf_op jit(solution)/shard_map/ppermute | solution.py:313
  95.3 7.6 %collective-permute-start.23 = (bf16[128,512]{1,0:T(8,128)(2,1)S(1)}, bf16[128,512]{1,0:T(8,128)(2,1)S(1)}, u32[]{:S(2)}, u32[]{:S(2)}) collective-permute-start(bf16[128,512]{1,0:T(8,128)(2,1)S(1)} %dynamic-slice_convert_fusion), channel_id=1, source_target_pairs={{0,1},{1,0},{2,3},{3,2},{4,5},{5,4},{6,7},{7,6},{8,9},{9,8},{10,11... | collective-permute-start | bytes 393224 | tf_op jit(solution)/shard_map/ppermute | solution.py:313
  (2 other events, 5.6 us)

commit v2 on v1

--- a/solution.py
+++ b/solution.py
@@ -277,7 +277,7 @@
 def weight_grad(left, right, keep, name):
     rows, height = left.shape
     width = right.shape[1]
-    tile = min(512, height)
+    tile = min(1024, height)
     flops = 2 * rows * height * width
     return pl.pallas_call(
         weight_grad_body,
@@ -289,7 +289,7 @@
         ],
         out_specs=pl.BlockSpec((tile, width), lambda i: (i, 0)),
         out_shape=jax.ShapeDtypeStruct((height, width), BF16),
-        compiler_params=pltpu.CompilerParams(vmem_limit_bytes=16 * 1024 * 1024),
+        compiler_params=pltpu.CompilerParams(vmem_limit_bytes=28 * 1024 * 1024),
         cost_estimate=pl.CostEstimate(flops=flops, bytes_accessed=flops // 256, transcendentals=0),
         name=name,
     )(left, right, keep)

time: 104 us -> 103 us (level)
  Pallas kernels: 47.8 us -> 46.6 us
where the time goes in v2:
time: 103 us
  Pallas kernels  46.6 us (45%)
  starting transfers between devices  41.2 us (40%)
  waiting for transfers between devices  8.18 us (8%)
  other arithmetic  4.72 us (5%)
  local copies, waits for them, and re-layouts  1.1 us (1%)
    pallas_call x4, Pallas kernels, call(): pl.pallas_call(body, grid=(1,), in_specs=[pl.BlockSpec(memory_space=pltpu...  28.3 us
    ppermute x7, starting transfers between devices, swap(): return lax.ppermute(part, 'dp', [(0, 1), (1, 0)])  26.5 us
    ppermute x17, starting transfers between devices, permute(): return lax.ppermute(x, ('tp', 'dp'), route)  14.7 us
    pallas_call x3, Pallas kernels, weight_grad(): pl.pallas_call(weight_grad_body, grid=(height // tile,), in_specs=[pl.Blo...  14.3 us
    ppermute x17, waiting for transfers between devices, permute(): return lax.ppermute(x, ('tp', 'dp'), route)  5.38 us
    pallas_call x1, Pallas kernels, prepare(): pl.pallas_call(prepare_body, grid=(rows // tile,), in_specs=[pl.BlockSpec...  3.98 us
    ppermute x7, waiting for transfers between devices, swap(): return lax.ppermute(part, 'dp', [(0, 1), (1, 0)])  2.81 us
  transfers between devices with their start and end apart: 24, of which 6 were waited for; matrix products, arithmetic and copies ran while one was open for 3% of the time, Pallas kernels for 38%

profile of v2, /device:TPU:19, one launch (start us, length us, event | category | flops | bytes accessed | tf_op | source)
XLA Modules:
  0.0 102.8 jit_solution(3282567617265817978)
XLA Ops:
  0.6 0.7 collective-permute-start
  1.4 1.2 %collective-permute-done = bf16[128,512]{1,0:T(8,128)(2,1)S(1)} collective-permute-done((bf16[128,512]{1,0:T(8,128)(2,1)}, bf16[128,512]{1,0:T(8,128)(2,1)S(1)}, u32[]{:S(2)}, u32[]{:S(2)}) %collective-permute-start) | collective-permute-done | bytes 131104 | tf_op jit(solution)/shard_map/ppermute | solution.py:313
  2.6 0.9 broadcast_select_fusion.4
  4.0 1.3 %collective-permute-start.5 = (bf16[256,512]{1,0:T(8,128)(2,1)S(1)}, bf16[256,512]{1,0:T(8,128)(2,1)S(1)}, u32[]{:S(2)}, u32[]{:S(2)}) collective-permute-start(bf16[256,512]{1,0:T(8,128)(2,1)S(1)} %pad_maximum_fusion.refs_0_), channel_id=1, source_target_pairs={{0,4},{1,12},{2,6},{3,14},{4,0},{5,8},{6,2},{7,10},{8,5},{9,13},{1... | collective-permute-start | bytes 786440 | tf_op jit(solution)/shard_map/ppermute | solution.py:305
  5.2 0.7 collective-permute-start.4
  5.9 0.9 broadcast_select_fusion.2
  6.9 0.7 collective-permute-start.3
  8.2 3.1 %collective-permute-start.6 = (bf16[256,512]{1,0:T(8,128)(2,1)S(1)}, bf16[256,512]{1,0:T(8,128)(2,1)S(1)}, u32[]{:S(2)}, u32[]{:S(2)}) collective-permute-start(bf16[256,512]{1,0:T(8,128)(2,1)S(1)} %pad_maximum_fusion.refs_0_), channel_id=1, source_target_pairs={{0,2},{2,0},{4,6},{6,4},{9,11},{11,9},{13,15},{15,13},{16,18},{18,... | collective-permute-start | bytes 786440 | tf_op jit(solution)/shard_map/ppermute | solution.py:305
  11.7 1.2 %collective-permute-start.7 = (bf16[256,512]{1,0:T(8,128)(2,1)S(1)}, bf16[256,512]{1,0:T(8,128)(2,1)S(1)}, u32[]{:S(2)}, u32[]{:S(2)}) collective-permute-start(bf16[256,512]{1,0:T(8,128)(2,1)S(1)} %collective-permute-done.5.refs_2_), channel_id=1, source_target_pairs={{0,2},{1,3},{2,0},{3,1},{4,6},{5,7},{6,4},{7,5},{8,10},{9,11},{10,... | collective-permute-start | bytes 786440 | tf_op jit(solution)/shard_map/ppermute | solution.py:305
  13.0 0.7 collective-permute-start.8
  14.0 3.6 %collective-permute-done.2.refs_1_ = bf16[256,512]{1,0:T(8,128)(2,1)S(1)} collective-permute-done((bf16[256,512]{1,0:T(8,128)(2,1)S(1)}, bf16[256,512]{1,0:T(8,128)(2,1)S(1)}, u32[]{:S(2)}, u32[]{:S(2)}) %collective-permute-start.2) | collective-permute-done | bytes 262176 | tf_op jit(solution)/shard_map/ppermute | solution.py:305
  17.6 1.2 %collective-permute-start.9 = (bf16[256,512]{1,0:T(8,128)(2,1)S(1)}, bf16[256,512]{1,0:T(8,128)(2,1)S(1)}, u32[]{:S(2)}, u32[]{:S(2)}) collective-permute-start(bf16[256,512]{1,0:T(8,128)(2,1)S(1)} %collective-permute-done.2.refs_1_), channel_id=1, source_target_pairs={{0,2},{1,3},{2,0},{3,1},{4,6},{5,7},{6,4},{7,5},{8,10},{9,11},{10,... | collective-permute-start | bytes 786440 | tf_op jit(solution)/shard_map/ppermute | solution.py:305
  18.9 0.8 dynamic-slice_convert_fusion.2
  20.1 8.2 %forward.1 = (bf16[256,2048]{1,0:T(8,128)(2,1)S(1)}, bf16[256,2048]{1,0:T(8,128)(2,1)S(1)}, bf16[256,2048]{1,0:T(8,128)(2,1)}) custom-call(s32[2]{0:T(128)S(1)} %pad_add_fusion.sel, bf16[2048,2048]{1,0:T(8,128)(2,1)} %refs_0_.3, bf16[2048,2048]{1,0:T(8,128)(2,1)} %refs_1_.3, f32[16,1,2048]{2,1,0:T(1,128)S(1)} %bitcast.9, f32[16,1,2048]{2,1,0:T(1,128)S(1)} %bitcast.5, ...), custom_call_target="tpu_custom_call" | custom-call | flops 67108864 | bytes 262144 | tf_op jit(solution)/shard_map/forward/pallas_call | solution.py:36
  28.4 12.3 %collective-permute-start.11 = (bf16[256,2048]{1,0:T(8,128)(2,1)S(1)}, bf16[256,2048]{1,0:T(8,128)(2,1)S(1)}, u32[]{:S(2)}, u32[]{:S(2)}) collective-permute-start(bf16[256,2048]{1,0:T(8,128)(2,1)S(1)} %get-tuple-element.41.refs_4_), channel_id=1, source_target_pairs={{0,1},{1,0},{2,3},{3,2},{4,5},{5,4},{6,7},{7,6},{8,9},{9,8},{10,11... | collective-permute-start | bytes 3145736 | tf_op jit(solution)/shard_map/ppermute | solution.py:313
  41.6 4.0 %prepare_down.1.weight = bf16[2048,2048]{1,0:T(8,128)(2,1)S(1)} custom-call(bf16[2048,2048]{1,0:T(8,128)(2,1)} %weight.1, f32[16,1,2048]{2,1,0:T(1,128)S(1)} %bitcast.13), custom_call_target="tpu_custom_call" | custom-call | bytes 262144 | tf_op jit(solution)/shard_map/prepare_down/pallas_call | solution.py:66
  45.6 8.0 %middle.1 = (bf16[256,2048]{1,0:T(8,128)(2,1)S(1)}, bf16[256,2048]{1,0:T(8,128)(2,1)}, bf16[256,2048]{1,0:T(8,128)(2,1)}, f32[256,2048]{1,0:T(8,128)S(1)}, f32[2...) custom-call(s32[2]{0:T(128)S(1)} %pad_add_fusion.sel, ...), custom_call_target="tpu_custom_call" | custom-call | flops 4294967296 | bytes 16777216 | tf_op jit(solution)/shard_map/middle/pallas_call | solution.py:36
  53.9 1.2 %collective-permute-start.17 = (bf16[256,512]{1,0:T(8,128)(2,1)}, bf16[256,512]{1,0:T(8,128)(2,1)S(1)}, u32[]{:S(2)}, u32[]{:S(2)}) collective-permute-start(bf16[256,512]{1,0:T(8,128)(2,1)} %get-tuple-element.59), channel_id=1, source_target_pairs={{0,2},{1,3},{2,0},{3,1},{4,6},{5,7},{6,4},{7,5},{8,10},{9,11},{10,... | collective-permute-start | bytes 786440 | tf_op jit(solution)/shard_map/ppermute | solution.py:305
  55.1 1.3 %collective-permute-done.14.refs_7_ = bf16[256,2048]{1,0:T(8,128)(2,1)} collective-permute-done((bf16[256,2048]{1,0:T(8,128)(2,1)S(1)}, bf16[256,2048]{1,0:T(8,128)(2,1)}, u32[]{:S(2)}, u32[]{:S(2)}) %collective-permute-start.14) | collective-permute-done | bytes 1048608 | tf_op jit(solution)/shard_map/ppermute | solution.py:313
  56.4 5.4 %input_first.1 = (bf16[256,512]{1,0:T(8,128)(2,1)S(1)}, bf16[256,2048]{1,0:T(8,128)(2,1)S(1)}, bf16[256,2048]{1,0:T(8,128)(2,1)S(1)}) custom-call(s32[2]{0:T(128)S(1)} %pad_add_fusion.sel, bf16[2048,2048]{1,0:T(8,128)(2,1)} %refs_0_.3, bf16[2048,2048]{1,0:T(8,128)(2,1)} %refs_1_.3, f32[16,1,2048]{2,1,0:T(1,128)S(1)} %bitcast.10, f32[16,1,2048]{2,1,0:T(1,128)S(1)} %bitcast.6, ...), custom_call_target="tpu_custom_call" | custom-call | flops 1073741824 | bytes 4194304 | tf_op jit(solution)/shard_map/input_first/pallas_call | solution.py:36
  62.1 6.7 %input_rest.1 = (bf16[256,512]{1,0:T(8,128)(2,1)S(1)}, bf16[256,512]{1,0:T(8,128)(2,1)S(1)}, bf16[256,512]{1,0:T(8,128)(2,1)S(1)}) custom-call(s32[2]{0:T(128)S(1)} %pad_add_fusion.sel, bf16[2048,2048]{1,0:T(8,128)(2,1)} %refs_0_.3, bf16[2048,2048]{1,0:T(8,128)(2,1)} %refs_1_.3, f32[16,1,2048]{2,1,0:T(1,128)S(1)} %bitcast.11, f32[16,1,2048]{2,1,0:T(1,128)S(1)} %bitcast.7, ...), custom_call_target="tpu_custom_call" | custom-call | flops 3221225472 | bytes 12582912 | tf_op jit(solution)/shard_map/input_rest/pallas_call | solution.py:36
  68.8 1.3 %collective-permute-start.20 = (bf16[256,512]{1,0:T(8,128)(2,1)S(1)}, bf16[256,512]{1,0:T(8,128)(2,1)S(1)}, u32[]{:S(2)}, u32[]{:S(2)}) collective-permute-start(bf16[256,512]{1,0:T(8,128)(2,1)S(1)} %get-tuple-element.62), channel_id=1, source_target_pairs={{0,2},{1,3},{2,0},{3,1},{4,6},{5,7},{6,4},{7,5},{8,10},{9,11},{10,... | collective-permute-start | bytes 786440 | tf_op jit(solution)/shard_map/ppermute | solution.py:305
  70.1 4.8 %gate_grad.1 = bf16[2048,2048]{1,0:T(8,128)(2,1)} custom-call(bf16[256,2048]{1,0:T(8,128)(2,1)S(1)} %copy-done, bf16[256,2048]{1,0:T(8,128)(2,1)S(1)} %get-tuple-element.50.refs_4_.right, f32[16,1,2048]{2,1,0:T(1,128)S(1)} %bitcast.12), custom_call_target="tpu_custom_call" | custom-call | flops 2147483648 | bytes 8388608 | tf_op jit(solution)/shard_map/gate_grad/pallas_call | solution.py:282
  75.2 0.8 collective-permute-start.18
  76.1 0.7 collective-permute-start.22
  76.7 1.3 %collective-permute-done.20 = bf16[256,512]{1,0:T(8,128)(2,1)S(1)} collective-permute-done((bf16[256,512]{1,0:T(8,128)(2,1)S(1)}, bf16[256,512]{1,0:T(8,128)(2,1)S(1)}, u32[]{:S(2)}, u32[]{:S(2)}) %collective-permute-start.20) | collective-permute-done | bytes 262176 | tf_op jit(solution)/shard_map/ppermute | solution.py:305
  78.1 4.8 %up_grad.1 = bf16[2048,2048]{1,0:T(8,128)(2,1)} custom-call(bf16[256,2048]{1,0:T(8,128)(2,1)S(1)} %copy-done, bf16[256,2048]{1,0:T(8,128)(2,1)S(1)} %get-tuple-element.64.refs_5_.right, f32[16,1,2048]{2,1,0:T(1,128)S(1)} %bitcast.8), custom_call_target="tpu_custom_call" | custom-call | flops 2147483648 | bytes 8388608 | tf_op jit(solution)/shard_map/up_grad/pallas_call | solution.py:282
  83.2 4.8 %down_grad.1 = bf16[2048,2048]{1,0:T(8,128)(2,1)} custom-call(bf16[256,2048]{1,0:T(8,128)(2,1)S(1)} %copy-done.2, bf16[256,2048]{1,0:T(8,128)(2,1)S(1)} %copy-done.1, f32[16,1,2048]{2,1,0:T(1,128)S(1)} %bitcast.14), custom_call_target="tpu_custom_call" | custom-call | flops 2147483648 | bytes 8388608 | tf_op jit(solution)/shard_map/down_grad/pallas_call | solution.py:282
  88.1 6.2 %collective-permute-start.19 = (bf16[128,512]{1,0:T(8,128)(2,1)S(1)}, bf16[128,512]{1,0:T(8,128)(2,1)S(1)}, u32[]{:S(2)}, u32[]{:S(2)}) collective-permute-start(bf16[128,512]{1,0:T(8,128)(2,1)S(1)} %dynamic-slice_convert_fusion.1), channel_id=1, source_target_pairs={{0,1},{1,0},{2,3},{3,2},{4,5},{5,4},{6,7},{7,6},{8,9},{9,8},{10,11... | collective-permute-start | bytes 393224 | tf_op jit(solution)/shard_map/ppermute | solution.py:313
  94.4 6.7 %collective-permute-start.23 = (bf16[128,512]{1,0:T(8,128)(2,1)S(1)}, bf16[128,512]{1,0:T(8,128)(2,1)S(1)}, u32[]{:S(2)}, u32[]{:S(2)}) collective-permute-start(bf16[128,512]{1,0:T(8,128)(2,1)S(1)} %dynamic-slice_convert_fusion), channel_id=1, source_target_pairs={{0,1},{1,0},{2,3},{3,2},{4,5},{5,4},{6,7},{7,6},{8,9},{9,8},{10,11... | collective-permute-start | bytes 393224 | tf_op jit(solution)/shard_map/ppermute | solution.py:313
  101.2 0.7 add_convert_fusion.5
  102.2 0.7 add_convert_fusion.4
  (67 shorter events, 4.9 us)
Async XLA Ops:
  0.6 1.9 %collective-permute-start = (bf16[128,512]{1,0:T(8,128)(2,1)}, bf16[128,512]{1,0:T(8,128)(2,1)S(1)}, u32[]{:S(2)}, u32[]{:S(2)}) collective-permute-start(bf16[128,512]{1,0:T(8,128)(2,1)} %param.8), channel_id=1, source_target_pairs={{0,1},{1,0},{2,3},{3,2},{4,5},{5,4},{6,7},{7,6},{8,9},{9,8},{10,11... | collective-permute-start | bytes 393224 | tf_op jit(solution)/shard_map/ppermute | solution.py:313
  3.5 2.4 %collective-permute-start.1 = (bf16[128,512]{1,0:T(8,128)(2,1)}, bf16[128,512]{1,0:T(8,128)(2,1)S(1)}, u32[]{:S(2)}, u32[]{:S(2)}) collective-permute-start(bf16[128,512]{1,0:T(8,128)(2,1)} %param.9), channel_id=1, source_target_pairs={{0,1},{1,0},{2,3},{3,2},{4,5},{5,4},{6,7},{7,6},{8,9},{9,8},{10,11... | collective-permute-start | bytes 393224 | tf_op jit(solution)/shard_map/ppermute | solution.py:313
  4.0 7.8 %collective-permute-start.5 = (bf16[256,512]{1,0:T(8,128)(2,1)S(1)}, bf16[256,512]{1,0:T(8,128)(2,1)S(1)}, u32[]{:S(2)}, u32[]{:S(2)}) collective-permute-start(bf16[256,512]{1,0:T(8,128)(2,1)S(1)} %pad_maximum_fusion.refs_0_), channel_id=1, source_target_pairs={{0,4},{1,12},{2,6},{3,14},{4,0},{5,8},{6,2},{7,10},{8,5},{9,13},{1... | collective-permute-start | bytes 786440 | tf_op jit(solution)/shard_map/ppermute | solution.py:305
  5.2 7.7 %collective-permute-start.4 = (bf16[256,512]{1,0:T(8,128)(2,1)S(1)}, bf16[256,512]{1,0:T(8,128)(2,1)S(1)}, u32[]{:S(2)}, u32[]{:S(2)}) collective-permute-start(bf16[256,512]{1,0:T(8,128)(2,1)S(1)} %pad_maximum_fusion.refs_0_), channel_id=1, source_target_pairs={{1,8},{3,10},{5,12},{7,14},{8,1},{10,3},{12,5},{14,7},{17,24},{19,... | collective-permute-start | bytes 786440 | tf_op jit(solution)/shard_map/ppermute | solution.py:305
  6.9 6.7 %collective-permute-start.3 = (bf16[256,512]{1,0:T(8,128)(2,1)S(1)}, bf16[256,512]{1,0:T(8,128)(2,1)S(1)}, u32[]{:S(2)}, u32[]{:S(2)}) collective-permute-start(bf16[256,512]{1,0:T(8,128)(2,1)S(1)} %pad_maximum_fusion.1), channel_id=1, source_target_pairs={{1,8},{3,10},{5,12},{7,14},{8,1},{10,3},{12,5},{14,7},{17,24},{19,... | collective-permute-start | bytes 786440 | tf_op jit(solution)/shard_map/ppermute | solution.py:305
  7.6 10.1 %collective-permute-start.2 = (bf16[256,512]{1,0:T(8,128)(2,1)S(1)}, bf16[256,512]{1,0:T(8,128)(2,1)S(1)}, u32[]{:S(2)}, u32[]{:S(2)}) collective-permute-start(bf16[256,512]{1,0:T(8,128)(2,1)S(1)} %pad_maximum_fusion.1), channel_id=1, source_target_pairs={{0,4},{1,12},{2,6},{3,14},{4,0},{5,8},{6,2},{7,10},{8,5},{9,13},{1... | collective-permute-start | bytes 786440 | tf_op jit(solution)/shard_map/ppermute | solution.py:305
  8.2 11.7 %collective-permute-start.6 = (bf16[256,512]{1,0:T(8,128)(2,1)S(1)}, bf16[256,512]{1,0:T(8,128)(2,1)S(1)}, u32[]{:S(2)}, u32[]{:S(2)}) collective-permute-start(bf16[256,512]{1,0:T(8,128)(2,1)S(1)} %pad_maximum_fusion.refs_0_), channel_id=1, source_target_pairs={{0,2},{2,0},{4,6},{6,4},{9,11},{11,9},{13,15},{15,13},{16,18},{18,... | collective-permute-start | bytes 786440 | tf_op jit(solution)/shard_map/ppermute | solution.py:305
  11.7 8.2 %collective-permute-start.7 = (bf16[256,512]{1,0:T(8,128)(2,1)S(1)}, bf16[256,512]{1,0:T(8,128)(2,1)S(1)}, u32[]{:S(2)}, u32[]{:S(2)}) collective-permute-start(bf16[256,512]{1,0:T(8,128)(2,1)S(1)} %collective-permute-done.5.refs_2_), channel_id=1, source_target_pairs={{0,2},{1,3},{2,0},{3,1},{4,6},{5,7},{6,4},{7,5},{8,10},{9,11},{10,... | collective-permute-start | bytes 786440 | tf_op jit(solution)/shard_map/ppermute | solution.py:305
  13.0 6.9 %collective-permute-start.8 = (bf16[256,512]{1,0:T(8,128)(2,1)S(1)}, bf16[256,512]{1,0:T(8,128)(2,1)S(1)}, u32[]{:S(2)}, u32[]{:S(2)}) collective-permute-start(bf16[256,512]{1,0:T(8,128)(2,1)S(1)} %collective-permute-done.4.refs_1_), channel_id=1, source_target_pairs={{1,3},{3,1},{5,7},{7,5},{8,10},{10,8},{12,14},{14,12},{17,19},{19,... | collective-permute-start | bytes 786440 | tf_op jit(solution)/shard_map/ppermute | solution.py:305
  13.7 14.6 %copy-start.5 = (bf16[256,512]{1,0:T(8,128)(2,1)}, bf16[256,512]{1,0:T(8,128)(2,1)S(1)}, u32[]{:S(2)}) copy-start(bf16[256,512]{1,0:T(8,128)(2,1)S(1)} %broadcast_select_fusion.refs_0_) | copy-start | bytes 786436
  13.7 26.9 %collective-permute-start.10 = (bf16[256,512]{1,0:T(8,128)(2,1)S(1)}, bf16[256,512]{1,0:T(8,128)(2,1)S(1)}, u32[]{:S(2)}, u32[]{:S(2)}) collective-permute-start(bf16[256,512]{1,0:T(8,128)(2,1)S(1)} %broadcast_select_fusion.refs_0_), channel_id=1, source_target_pairs={{0,2},{1,3},{2,0},{3,1},{4,6},{5,7},{6,4},{7,5},{8,10},{9,11},{10,... | collective-permute-start | bytes 786440 | tf_op jit(solution)/shard_map/ppermute | solution.py:305
  17.6 10.7 %copy-start.7 = (bf16[256,512]{1,0:T(8,128)(2,1)}, bf16[256,512]{1,0:T(8,128)(2,1)S(1)}, u32[]{:S(2)}) copy-start(bf16[256,512]{1,0:T(8,128)(2,1)S(1)} %collective-permute-done.2.refs_1_) | copy-start | bytes 786436
  17.6 23.0 %collective-permute-start.9 = (bf16[256,512]{1,0:T(8,128)(2,1)S(1)}, bf16[256,512]{1,0:T(8,128)(2,1)S(1)}, u32[]{:S(2)}, u32[]{:S(2)}) collective-permute-start(bf16[256,512]{1,0:T(8,128)(2,1)S(1)} %collective-permute-done.2.refs_1_), channel_id=1, source_target_pairs={{0,2},{1,3},{2,0},{3,1},{4,6},{5,7},{6,4},{7,5},{8,10},{9,11},{10,... | collective-permute-start | bytes 786440 | tf_op jit(solution)/shard_map/ppermute | solution.py:305
  20.1 21.3 %copy-start.6 = (s32[16,32]{1,0:T(8,128)S(1)}, s32[16,32]{1,0:T(8,128)}, u32[]{:S(2)}) copy-start(s32[16,32]{1,0:T(8,128)} %param.15) | copy-start | bytes 6148
  28.4 17.2 %collective-permute-start.11 = (bf16[256,2048]{1,0:T(8,128)(2,1)S(1)}, bf16[256,2048]{1,0:T(8,128)(2,1)S(1)}, u32[]{:S(2)}, u32[]{:S(2)}) collective-permute-start(bf16[256,2048]{1,0:T(8,128)(2,1)S(1)} %get-tuple-element.41.refs_4_), channel_id=1, source_target_pairs={{0,1},{1,0},{2,3},{3,2},{4,5},{5,4},{6,7},{7,6},{8,9},{9,8},{10,11... | collective-permute-start | bytes 3145736 | tf_op jit(solution)/shard_map/ppermute | solution.py:313
  40.7 4.9 %collective-permute-start.12 = (bf16[256,2048]{1,0:T(8,128)(2,1)S(1)}, bf16[256,2048]{1,0:T(8,128)(2,1)S(1)}, u32[]{:S(2)}, u32[]{:S(2)}) collective-permute-start(bf16[256,2048]{1,0:T(8,128)(2,1)S(1)} %get-tuple-element.44.refs_6_), channel_id=1, source_target_pairs={{0,1},{1,0},{2,3},{3,2},{4,5},{5,4},{6,7},{7,6},{8,9},{9,8},{10,11... | collective-permute-start | bytes 3145736 | tf_op jit(solution)/shard_map/ppermute | solution.py:313
  53.6 2.8 %collective-permute-start.14 = (bf16[256,2048]{1,0:T(8,128)(2,1)S(1)}, bf16[256,2048]{1,0:T(8,128)(2,1)}, u32[]{:S(2)}, u32[]{:S(2)}) collective-permute-start(bf16[256,2048]{1,0:T(8,128)(2,1)S(1)} %get-tuple-element.49.refs_6_), channel_id=1, source_target_pairs={{0,1},{1,0},{2,3},{3,2},{4,5},{5,4},{6,7},{7,6},{8,9},{9,8},{10,11... | collective-permute-start | bytes 3145736 | tf_op jit(solution)/shard_map/ppermute | solution.py:313
  53.6 21.4 %collective-permute-start.13 = (bf16[256,512]{1,0:T(8,128)(2,1)}, bf16[256,512]{1,0:T(8,128)(2,1)S(1)}, u32[]{:S(2)}, u32[]{:S(2)}) collective-permute-start(bf16[256,512]{1,0:T(8,128)(2,1)} %get-tuple-element.46), channel_id=1, source_target_pairs={{0,2},{1,3},{2,0},{3,1},{4,6},{5,7},{6,4},{7,5},{8,10},{9,11},{10,... | collective-permute-start | bytes 786440 | tf_op jit(solution)/shard_map/ppermute | solution.py:305
  53.9 21.2 %collective-permute-start.17 = (bf16[256,512]{1,0:T(8,128)(2,1)}, bf16[256,512]{1,0:T(8,128)(2,1)S(1)}, u32[]{:S(2)}, u32[]{:S(2)}) collective-permute-start(bf16[256,512]{1,0:T(8,128)(2,1)} %get-tuple-element.59), channel_id=1, source_target_pairs={{0,2},{1,3},{2,0},{3,1},{4,6},{5,7},{6,4},{7,5},{8,10},{9,11},{10,... | collective-permute-start | bytes 786440 | tf_op jit(solution)/shard_map/ppermute | solution.py:305
  61.8 13.1 %collective-permute-start.15 = (bf16[256,512]{1,0:T(8,128)(2,1)S(1)}, bf16[256,512]{1,0:T(8,128)(2,1)S(1)}, u32[]{:S(2)}, u32[]{:S(2)}) collective-permute-start(bf16[256,512]{1,0:T(8,128)(2,1)S(1)} %get-tuple-element.53), channel_id=1, source_target_pairs={{0,2},{1,3},{2,0},{3,1},{4,6},{5,7},{6,4},{7,5},{8,10},{9,11},{10,... | collective-permute-start | bytes 786440 | tf_op jit(solution)/shard_map/ppermute | solution.py:305
  62.1 8.0 %copy-start = (bf16[256,2048]{1,0:T(8,128)(2,1)S(1)}, bf16[256,2048]{1,0:T(8,128)(2,1)}, u32[]{:S(2)}) copy-start(bf16[256,2048]{1,0:T(8,128)(2,1)} %get-tuple-element.55.left) | copy-start | bytes 3145732
  68.8 6.2 %copy-start.4 = (bf16[256,512]{1,0:T(8,128)(2,1)S(1)}, bf16[256,512]{1,0:T(8,128)(2,1)}, u32[]{:S(2)}) copy-start(bf16[256,512]{1,0:T(8,128)(2,1)} %get-tuple-element.45) | copy-start | bytes 786436
  68.8 6.3 %copy-start.3 = (bf16[256,512]{1,0:T(8,128)(2,1)S(1)}, bf16[256,512]{1,0:T(8,128)(2,1)}, u32[]{:S(2)}) copy-start(bf16[256,512]{1,0:T(8,128)(2,1)} %get-tuple-element.58) | copy-start | bytes 786436
  68.8 9.2 %collective-permute-start.20 = (bf16[256,512]{1,0:T(8,128)(2,1)S(1)}, bf16[256,512]{1,0:T(8,128)(2,1)S(1)}, u32[]{:S(2)}, u32[]{:S(2)}) collective-permute-start(bf16[256,512]{1,0:T(8,128)(2,1)S(1)} %get-tuple-element.62), channel_id=1, source_target_pairs={{0,2},{1,3},{2,0},{3,1},{4,6},{5,7},{6,4},{7,5},{8,10},{9,11},{10,... | collective-permute-start | bytes 786440 | tf_op jit(solution)/shard_map/ppermute | solution.py:305
  74.9 8.3 %copy-start.1 = (bf16[256,2048]{1,0:T(8,128)(2,1)S(1)}, bf16[256,2048]{1,0:T(8,128)(2,1)}, u32[]{:S(2)}) copy-start(bf16[256,2048]{1,0:T(8,128)(2,1)} %get-tuple-element.68.right) | copy-start | bytes 3145732
  74.9 8.3 %copy-start.2 = (bf16[256,2048]{1,0:T(8,128)(2,1)S(1)}, bf16[256,2048]{1,0:T(8,128)(2,1)}, u32[]{:S(2)}) copy-start(bf16[256,2048]{1,0:T(8,128)(2,1)} %get-tuple-element.66.left) | copy-start | bytes 3145732
  75.1 12.9 %collective-permute-start.16 = (bf16[256,512]{1,0:T(8,128)(2,1)S(1)}, bf16[256,512]{1,0:T(8,128)(2,1)S(1)}, u32[]{:S(2)}, u32[]{:S(2)}) collective-permute-start(bf16[256,512]{1,0:T(8,128)(2,1)S(1)} %add_convert_fusion.2), channel_id=1, source_target_pairs={{4,0},{12,1},{6,2},{14,3},{0,4},{8,5},{2,6},{10,7},{5,8},{13,9},{7... | collective-permute-start | bytes 786440 | tf_op jit(solution)/shard_map/ppermute | solution.py:305
  75.2 12.7 %collective-permute-start.18 = (bf16[256,512]{1,0:T(8,128)(2,1)S(1)}, bf16[256,512]{1,0:T(8,128)(2,1)S(1)}, u32[]{:S(2)}, u32[]{:S(2)}) collective-permute-start(bf16[256,512]{1,0:T(8,128)(2,1)S(1)} %add_convert_fusion.1), channel_id=1, source_target_pairs={{8,1},{10,3},{12,5},{14,7},{1,8},{3,10},{5,12},{7,14},{24,17},{26,... | collective-permute-start | bytes 786440 | tf_op jit(solution)/shard_map/ppermute | solution.py:305
  76.1 18.2 %collective-permute-start.22 = (bf16[256,512]{1,0:T(8,128)(2,1)S(1)}, bf16[256,512]{1,0:T(8,128)(2,1)S(1)}, u32[]{:S(2)}, u32[]{:S(2)}) collective-permute-start(bf16[256,512]{1,0:T(8,128)(2,1)S(1)} %add_convert_fusion.3), channel_id=1, source_target_pairs={{8,1},{10,3},{12,5},{14,7},{1,8},{3,10},{5,12},{7,14},{24,17},{26,... | collective-permute-start | bytes 786440 | tf_op jit(solution)/shard_map/ppermute | solution.py:305
  82.9 11.4 %collective-permute-start.21 = (bf16[256,512]{1,0:T(8,128)(2,1)S(1)}, bf16[256,512]{1,0:T(8,128)(2,1)S(1)}, u32[]{:S(2)}, u32[]{:S(2)}) collective-permute-start(bf16[256,512]{1,0:T(8,128)(2,1)S(1)} %add_convert_fusion), channel_id=1, source_target_pairs={{4,0},{12,1},{6,2},{14,3},{0,4},{8,5},{2,6},{10,7},{5,8},{13,9},{7... | collective-permute-start | bytes 786440 | tf_op jit(solution)/shard_map/ppermute | solution.py:305
  88.1 13.1 %collective-permute-start.19 = (bf16[128,512]{1,0:T(8,128)(2,1)S(1)}, bf16[128,512]{1,0:T(8,128)(2,1)S(1)}, u32[]{:S(2)}, u32[]{:S(2)}) collective-permute-start(bf16[128,512]{1,0:T(8,128)(2,1)S(1)} %dynamic-slice_convert_fusion.1), channel_id=1, source_target_pairs={{0,1},{1,0},{2,3},{3,2},{4,5},{5,4},{6,7},{7,6},{8,9},{9,8},{10,11... | collective-permute-start | bytes 393224 | tf_op jit(solution)/shard_map/ppermute | solution.py:313
  94.4 7.7 %collective-permute-start.23 = (bf16[128,512]{1,0:T(8,128)(2,1)S(1)}, bf16[128,512]{1,0:T(8,128)(2,1)S(1)}, u32[]{:S(2)}, u32[]{:S(2)}) collective-permute-start(bf16[128,512]{1,0:T(8,128)(2,1)S(1)} %dynamic-slice_convert_fusion), channel_id=1, source_target_pairs={{0,1},{1,0},{2,3},{3,2},{4,5},{5,4},{6,7},{7,6},{8,9},{9,8},{10,11... | collective-permute-start | bytes 393224 | tf_op jit(solution)/shard_map/ppermute | solution.py:313
  (2 other events, 5.6 us)
